TPU v7x, 256 devices: a whole 4x4x8 slice. The times are simulated.
256 devices in a mesh: gx: 8 (over y, core), gz: 32 (over x, z).
Axes of the slice: x: 4, y: 4, z: 8, core: 2. Of those that a mesh axis runs over, the one named last changes fastest.
Arguments:
- velocity: float32 [3, 64, 256, 128], P(None, 'gx', 'gz'), may hold values from -6 to 6
- spacing: float32 [129], replicated, may hold values from 0.5 to 2
- basis: bfloat16 [128, 3, 64, 256, 128], P(None, None, 'gx', 'gz')
- history: bfloat16 [40, 3, 64, 256, 128], P(None, None, 'gx', 'gz')
- picks: int32 [31], replicated, may hold values from 0 to 39, as said below
Outputs:
- velocity_new: float32 [3, 64, 256, 128], P(None, 'gx', 'gz')
- factor: float32 [160, 160], replicated
- directions: bfloat16 [32, 3, 64, 256, 128], P(None, None, 'gx', 'gz')
Inputs may be any that keep to these rules, and one draw needn't show every extreme that they name: `picks`: 31 distinct indices that always include 0 and 39.
All inputs are finite; a program needn't handle non-finite values.
Results may differ from a plain program's by a relative error of at most 0.0024.
The roundings to bfloat16 on the way count: a program that leaves them out, or rounds other values in their place, can miss the bound.
Values sent between devices are 32-bit elements; how exact they have to be, the bound alone decides.
No kernel may reach another device: no remote copies, remote signals or barrier semaphores. Data moves between devices by JAX's collectives and lax.ppermute only.
A program may use at most 192 MiB of HBM per device.

v0:
```python
import jax
import jax.numpy as jnp
from jax import lax
from jax.sharding import PartitionSpec as P

step_size = 0.1
viscosity = 0.05
forcing = 0.5
gammas = (8.0 / 15.0, 5.0 / 12.0, 3.0 / 4.0)
zetas = (0.0, -17.0 / 60.0, -5.0 / 12.0)


def extended(shard, sides, width):
    for axis, dim in sides:
        count, length = (lax.axis_size(axis), shard.shape[dim])
        up = [(i, (i + 1) % count) for i in range(count)]
        down = [(j, i) for i, j in up]
        last = lax.slice_in_dim(shard, length - width, length, axis=dim)
        first = lax.slice_in_dim(shard, 0, width, axis=dim)
        before = lax.ppermute(last, axis, up)
        after = lax.ppermute(first, axis, down)
        shard = jnp.concatenate([before, shard, after], axis=dim)
    return shard


def tendency(center, along_x, along_z, spacing):
    back_far, back_near, ahead_near, ahead_far = along_x
    side_far, side_near, front_near, front_far = along_z
    lower_gap = spacing[:-1]
    upper_gap = spacing[1:]
    padded_y = jnp.pad(center, ((0, 0), (0, 0), (0, 0), (1, 1)))
    beneath = padded_y[..., :-2]
    overhead = padded_y[..., 2:]
    grad_x = (8.0 * (ahead_near - back_near) - (ahead_far - back_far)) / 12.0
    grad_z = (8.0 * (front_near - side_near) - (front_far - side_far)) / 12.0
    grad_y = (overhead - beneath) / (lower_gap + upper_gap)
    curv_x = (-ahead_far + 16.0 * ahead_near - 30.0 * center + 16.0 * back_near - back_far) / 12.0
    curv_z = (-front_far + 16.0 * front_near - 30.0 * center + 16.0 * side_near - side_far) / 12.0
    curv_y = (
        2.0
        * ((overhead - center) / upper_gap - (center - beneath) / lower_gap)
        / (lower_gap + upper_gap)
    )
    advect = center[0:1] * grad_x + center[1:2] * grad_y + center[2:3] * grad_z
    push = jnp.array([forcing, 0.0, 0.0], jnp.float32)[:, None, None, None]
    return -advect + viscosity * (curv_x + curv_y + curv_z) + push


def inner(left, right):
    return lax.dot_general(
        left, right, (((1,), (1,)), ((), ())), preferred_element_type=jnp.float32
    )


def exact_dot(left, right):
    return jnp.dot(left, right, precision=lax.Precision.HIGHEST)


def upper_factor(gram):
    order = gram.shape[0]
    positions = jnp.arange(order, dtype=jnp.int32)

    def column_step(index, lower):
        done_row = lax.dynamic_slice_in_dim(lower, index, 1, 0)[0]
        column = lax.dynamic_slice_in_dim(gram, index, 1, 1)[:, 0]
        remain = column - exact_dot(lower, done_row)
        pivot_value = jnp.sqrt(lax.dynamic_slice_in_dim(remain, index, 1, 0)[0])
        new_column = jnp.where(positions >= index, remain / pivot_value, 0.0)
        marker = (positions == index).astype(jnp.float32)
        return lower + new_column[:, None] * marker[None, :]

    lower = lax.fori_loop(0, order, column_step, jnp.zeros((order, order), jnp.float32))
    return lower.T


def upper_inverse(factor):
    lower = factor.T
    order = lower.shape[0]
    positions = jnp.arange(order, dtype=jnp.int32)

    def row_step(index, solved):
        lower_row = lax.dynamic_slice_in_dim(lower, index, 1, 0)[0]
        diag_value = lax.dynamic_slice_in_dim(lower_row, index, 1, 0)[0]
        marker = (positions == index).astype(jnp.float32)
        new_row = (marker - exact_dot(lower_row, solved)) / diag_value
        return solved + marker[:, None] * new_row[None, :]

    solved = lax.fori_loop(0, order, row_step, jnp.zeros((order, order), jnp.float32))
    return solved.T


def body(velocity, spacing, basis, history, picks):
    width_x = velocity.shape[1]
    width_z = velocity.shape[2]
    field = velocity
    previous = jnp.zeros_like(velocity)
    for section in range(3):
        padded = extended(field, (("gx", 1), ("gz", 2)), 2)
        along_x = tuple(
            (padded[:, start : start + width_x, 2 : 2 + width_z] for start in (0, 1, 3, 4))
        )
        along_z = tuple(
            (padded[:, 2 : 2 + width_x, start : start + width_z] for start in (0, 1, 3, 4))
        )
        current = tendency(field, along_x, along_z, spacing)
        field = field + step_size * (gammas[section] * current + zetas[section] * previous)
        previous = current
    fresh = field.astype(jnp.bfloat16)
    rank = basis.shape[0]
    stored = history.shape[0]
    snaps = picks.shape[0] + 1
    basis_flat = basis.reshape(rank, -1)
    stored_flat = history.reshape(stored, -1)
    fresh_flat = fresh.reshape(1, -1)
    rows = basis_flat.shape[1] * lax.axis_size("gx") * lax.axis_size("gz")
    cross_bb = inner(basis_flat, basis_flat)
    cross_bh = inner(basis_flat, stored_flat)
    cross_bf = inner(basis_flat, fresh_flat)
    cross_hh = inner(stored_flat, stored_flat)
    cross_hf = inner(stored_flat, fresh_flat)
    cross_ff = inner(fresh_flat, fresh_flat)
    full = jnp.block(
        [
            [cross_bb, cross_bh, cross_bf],
            [cross_bh.T, cross_hh, cross_hf],
            [cross_bf.T, cross_hf.T, cross_ff],
        ]
    )
    total = rank + stored + 1
    indices = jnp.concatenate(
        [jnp.arange(rank, dtype=jnp.int32), rank + picks, jnp.array([rank + stored], jnp.int32)]
    )
    select = (indices[:, None] == jnp.arange(total, dtype=jnp.int32)[None, :]).astype(jnp.float32)
    local = exact_dot(exact_dot(select, full), select.T)
    gram = lax.psum(local, ("gx", "gz")) / rows
    factor = upper_factor(gram)
    inverse = upper_inverse(factor)
    rounded = inverse.astype(jnp.bfloat16)
    part_basis = rounded[:rank, rank:]
    part_snap = rounded[rank:, rank:]
    placing = (picks[:, None] == jnp.arange(stored, dtype=jnp.int32)[None, :]).astype(jnp.float32)
    stored_coef = exact_dot(placing.T, part_snap[:-1].astype(jnp.float32)).astype(jnp.bfloat16)
    fresh_coef = part_snap[-1:]
    directions = jnp.dot(part_basis.T, basis_flat, preferred_element_type=jnp.float32)
    directions = directions + jnp.dot(
        stored_coef.T, stored_flat, preferred_element_type=jnp.float32
    )
    directions = directions + jnp.dot(fresh_coef.T, fresh_flat, preferred_element_type=jnp.float32)
    directions = directions.astype(jnp.bfloat16).reshape((snaps,) + velocity.shape)
    return (field, factor, directions)


def solution(mesh):
    return jax.shard_map(
        body,
        mesh=mesh,
        in_specs=(
            P(None, "gx", "gz", None),
            P(),
            P(None, None, "gx", "gz", None),
            P(None, None, "gx", "gz", None),
            P(),
        ),
        out_specs=(P(None, "gx", "gz", None), P(), P(None, None, "gx", "gz", None)),
        check_vma=False,
    )
```

profile of v0, /device:TPU:1, one launch (start us, length us, event | category | flops | bytes accessed | tf_op | source)
XLA Modules:
  0.0 864.0 jit_solution(5112864820208237519)
XLA Ops:
  7.2 0.8 fusion.82
  8.0 2.7 collective-permute-start.1
  11.2 9.1 %copy.25 = bf16[128,3,8,8,128]{0,4,3,2,1:T(8,128)(2,1)} copy(bf16[128,3,8,8,128]{4,3,2,1,0:T(8,128)(2,1)} %param.15) | data formatting | bytes 12582912 | tf_op args[2]
  20.4 7.5 fusion.21
  27.9 2.3 fusion.38
  30.2 4.2 fusion.35
  34.6 7.6 collective-permute-start.2
  42.3 1.0 collective-permute-done.2
  43.3 5.1 collective-permute-done.3
  48.6 3.1 collective-permute-start.4
  51.7 1.5 collective-permute-done.4
  53.2 1.5 collective-permute-start.7
  54.7 1.3 collective-permute-done.6
  56.0 3.4 collective-permute-done.7
  59.7 4.2 collective-permute-start.8
  64.1 0.7 collective-permute-done.8
  65.2 1.5 collective-permute-start.11
  66.7 1.3 collective-permute-done.10
  68.0 3.6 collective-permute-done.11
  72.5 3.8 fusion.67
  76.3 1.3 fusion.27
  77.8 1.0 fusion.41
  78.8 1.0 fusion.59
  79.8 238.8 %all-reduce.5.cloned.1.call-done = f32[160,160]{1,0:T(8,128)} async-done(((f32[160,160]{1,0:T(8,128)}), f32[160,160]{1,0:T(8,128)}) %all-reduce.5.cloned.1.call-update) | async-done | bytes 102416 | tf_op jit(solution)/shard_map/psum | solution.py:135
  318.6 0.9 broadcast_multiply_fusion
  319.7 276.0 %while.33 = (s32[]{:T(128)}, f32[160,160]{1,0:T(8,128)S(1)}, f32[160,160]{0,1:T(8,128)S(1)}, s32[]{:T(128)}, s32[]{:T(128)}) while((s32[]{:T(128)}, f32[160,160]{1,0:T(8,128)S(1)}, f32[160,160]{0,1:T(8,128)S(1)}, s32[]{:T(128)}, s32[]{:T(128)}) %tuple.100), condition=%wide.region_2.3_spmd.clone.clone, body=%wide.region_1.2_spmd.clone.clone.sunk | while | flops 410563 | bytes 581616 | solution.py:72
  595.7 250.0 %while.32 = (s32[]{:T(128)}, f32[160,160]{1,0:T(8,128)S(1)}, f32[160,160]{1,0:T(8,128)S(1)}, s32[]{:T(128)}, s32[]{:T(128)}, /*index=5*/s32[]{:T(128)}) while((s32[]{:T(128)}, f32[160,160]{1,0:T(8,128)S(1)}, f32[160,160]{1,0:T(8,128)S(1)}, s32[]{:T(128)}, s32[]{:T(128)}, /*index=5*/s32[]{:T(128)}) %tuple.103), condition=%wide.region_4.5_spmd.clone, body=%wide.region_3.4_spmd.clone.sunk | while | flops 410564 | bytes 373628 | solution.py:88
  596.5 0.6 subtract_divide_fusion.2
  846.2 0.8 copy.24
  847.0 6.7 fusion.18
  853.7 2.0 fusion.32
  855.7 1.5 copy.37
  (2135 shorter events, 401.4 us)
Async XLA Ops:
  7.2 311.5 %all-reduce.5.cloned.1.call-start = ((), (), s32[]{:S(2)}) async-start(), calls=%async_computation | async-start | bytes 327680 | tf_op jit(solution)/shard_map/psum | solution.py:135
  8.0 26.5 %collective-permute-start.1 = (f32[3,2,8,128]{3,2,1,0:T(8,128)S(1)}, f32[3,2,8,128]{3,2,1,0:T(8,128)S(1)}, u32[]{:S(2)}, u32[]{:S(2)}) collective-permute-start(f32[3,2,8,128]{3,2,1,0:T(8,128)S(1)} %get-tuple-element.297), channel_id=1, source_target_pairs={{0,32},{32,64},{64,96},{96,128},{128,160},{160,192},{192,224},{224... | collective-permute-start | bytes 73736 | tf_op jit(solution)/shard_map/ppermute | solution.py:20
  10.7 9.7 %copy-start.3 = (bf16[40,3,8,8,128]{4,3,2,1,0:T(8,128)(2,1)S(1)}, bf16[40,3,8,8,128]{4,3,2,1,0:T(8,128)(2,1)}, u32[]{:S(2)}) copy-start(bf16[40,3,8,8,128]{4,3,2,1,0:T(8,128)(2,1)} %param.16) | copy-start | bytes 5898244
  10.7 23.9 %collective-permute-start = (f32[3,2,8,128]{3,2,1,0:T(8,128)S(1)}, f32[3,2,8,128]{3,2,1,0:T(8,128)S(1)}, u32[]{:S(2)}, u32[]{:S(2)}) collective-permute-start(f32[3,2,8,128]{3,2,1,0:T(8,128)S(1)} %get-tuple-element.296), channel_id=1, source_target_pairs={{32,0},{64,32},{96,64},{128,96},{160,128},{192,160},{224,192},{0,2... | collective-permute-start | bytes 73736 | tf_op jit(solution)/shard_map/ppermute | solution.py:21
  20.3 9.8 %copy-start = (bf16[128,3,8,8,128]{0,4,3,2,1:T(8,128)(2,1)S(1)}, bf16[128,3,8,8,128]{0,4,3,2,1:T(8,128)(2,1)}, u32[]{:S(2)}) copy-start(bf16[128,3,8,8,128]{0,4,3,2,1:T(8,128)(2,1)} %copy.25) | copy-start | bytes 18874372
  20.4 9.8 %copy-start.1 = (bf16[128,3,8,8,128]{4,3,2,1,0:T(8,128)(2,1)S(1)}, bf16[128,3,8,8,128]{4,3,2,1,0:T(8,128)(2,1)}, u32[]{:S(2)}) copy-start(bf16[128,3,8,8,128]{4,3,2,1,0:T(8,128)(2,1)} %param.15) | copy-start | bytes 18874372
  30.2 4.3 copy-start.2
  30.2 12.0 %copy-start.6 = (f32[129]{0:T(256)S(1)}, f32[129]{0:T(256)}, u32[]{:S(2)}) copy-start(f32[129]{0:T(256)} %param.14) | copy-start | bytes 1552
  30.2 18.1 %copy-start.5 = (f32[3]{0:T(128)S(1)}, f32[3]{0:T(128)}, u32[]{:S(2)}) copy-start(f32[3]{0:T(128)} %constant.162.clone) | copy-start | bytes 40
  30.2 21.4 %copy-start.7 = (s32[31]{0:T(128)S(1)}, s32[31]{0:T(128)}, u32[]{:S(2)}) copy-start(s32[31]{0:T(128)} %param.17) | copy-start | bytes 376
  34.6 8.6 collective-permute-start.2
  42.2 6.1 collective-permute-start.3
  48.6 4.6 collective-permute-start.4
  51.6 1.5 collective-permute-start.5
  53.2 2.9 collective-permute-start.6
  53.2 6.2 collective-permute-start.7
  59.7 5.0 collective-permute-start.8
  63.9 1.2 collective-permute-start.9
  65.1 2.9 collective-permute-start.10
  65.2 6.4 collective-permute-start.11
  71.9 4.4 copy-start.4
Sparse Core Ops, SparseCore 0:
  79.9 238.6 all-reduce.4
where the time goes:
time: 867 us; the launch traced here: 864 us
  waiting for transfers between devices  257 us (30%)
  local copies, waits for them, and re-layouts  213 us (25%)
  other arithmetic  142 us (16%)
  loops' own time  128 us (15%)
  matrix products  88.2 us (10%)
  starting transfers between devices  21.2 us (2%)
  between operations  14.3 us (2%)
    psum x1, waiting for transfers between devices, body(): gram = lax.psum(local, ('gx', 'gz')) / rows  239 us
    another operation x1, loops' own time, upper_factor(): lax.fori_loop(0, order, column_step, jnp.zeros((order, order), jnp.float32))  121 us
    div x160, other arithmetic, row_step(): new_row = (marker - exact_dot(lower_row, solved)) / diag_value  104 us
    dynamic_slice x160, local copies, waits for them, and re-layouts, row_step(): diag_value = lax.dynamic_slice_in_dim(lower_row, index, 1, 0)[0]  96.6 us
    dynamic_slice x160, local copies, waits for them, and re-layouts, column_step(): pivot_value = jnp.sqrt(lax.dynamic_slice_in_dim(remain, index, 1, 0)[0])  94.2 us
    dot_general x323, matrix products, exact_dot(): return jnp.dot(left, right, precision=lax.Precision.HIGHEST)  60.4 us
    dot_general x5, matrix products, inner(): lax.dot_general(left, right, (((1,), (1,)), ((), ())), preferred_element_...  19.1 us
  transfers between devices with their start and end apart: 13, of which 10 were waited for; matrix products, arithmetic and copies ran while one was open for 3% of the time, Pallas kernels for 0%

commit v1 on v0

--- a/solution.py
+++ b/solution.py
@@ -1,6 +1,8 @@
 import jax
 import jax.numpy as jnp
 from jax import lax
+from jax.experimental import pallas as pl
+from jax.experimental.pallas import tpu as pltpu
 from jax.sharding import PartitionSpec as P
 
 step_size = 0.1
@@ -56,54 +58,151 @@
     return jnp.dot(left, right, precision=lax.Precision.HIGHEST)
 
 
-def upper_factor(gram):
-    order = gram.shape[0]
-    positions = jnp.arange(order, dtype=jnp.int32)
-
-    def column_step(index, lower):
-        done_row = lax.dynamic_slice_in_dim(lower, index, 1, 0)[0]
-        column = lax.dynamic_slice_in_dim(gram, index, 1, 1)[:, 0]
-        remain = column - exact_dot(lower, done_row)
-        pivot_value = jnp.sqrt(lax.dynamic_slice_in_dim(remain, index, 1, 0)[0])
-        new_column = jnp.where(positions >= index, remain / pivot_value, 0.0)
-        marker = (positions == index).astype(jnp.float32)
-        return lower + new_column[:, None] * marker[None, :]
-
-    lower = lax.fori_loop(0, order, column_step, jnp.zeros((order, order), jnp.float32))
-    return lower.T
-
-
-def upper_inverse(factor):
-    lower = factor.T
-    order = lower.shape[0]
-    positions = jnp.arange(order, dtype=jnp.int32)
-
-    def row_step(index, solved):
-        lower_row = lax.dynamic_slice_in_dim(lower, index, 1, 0)[0]
-        diag_value = lax.dynamic_slice_in_dim(lower_row, index, 1, 0)[0]
-        marker = (positions == index).astype(jnp.float32)
-        new_row = (marker - exact_dot(lower_row, solved)) / diag_value
-        return solved + marker[:, None] * new_row[None, :]
-
-    solved = lax.fori_loop(0, order, row_step, jnp.zeros((order, order), jnp.float32))
-    return solved.T
+places = {(i, j): (i, j) for i in range(4) for j in range(i, 4)}
+places.update({(4, 4): (1, 0), (2, 4): (2, 0), (3, 4): (2, 1), (0, 4): (3, 0), (1, 4): (3, 1)})
+
+
+def factor_kernel(packed_ref, factor_ref, left_ref, right_ref, work, side):
+    f32 = jnp.float32
+    lanes8 = lax.broadcasted_iota(jnp.int32, (8, 128), 1)
+    subs8 = lax.broadcasted_iota(jnp.int32, (8, 128), 0)
+    lanes = lax.broadcasted_iota(jnp.int32, (32, 128), 1)
+    rows = lax.broadcasted_iota(jnp.int32, (32, 128), 0)
+    for p in range(4):
+        piece = packed_ref[32 * p : 32 * p + 32, :]
+        work[32 * p : 32 * p + 32, :] = jnp.where(lanes >= 32 * p, piece, 0.0)
+        r, c = places[(p, 4)]
+        last = packed_ref[32 * r : 32 * r + 32, :]
+        if c:
+            last = pltpu.roll(last, 128 - 32 * c, 1)
+        side[32 * p : 32 * p + 32, :] = jnp.where(lanes < 32, last, 0.0)
+    r, c = places[(4, 4)]
+    work[128:160, :] = jnp.zeros((32, 128), f32)
+    side[128:160, :] = jnp.where(lanes < 32, packed_ref[32 * r : 32 * r + 32, :], 0.0)
+
+    for p in range(5):
+        base = 32 * p
+        main = [work[base + 8 * g : base + 8 * g + 8, :] for g in range(4)]
+        tail = [side[base + 8 * g : base + 8 * g + 8, :] for g in range(4)]
+        scale = [None] * 4
+        for gk in range(4):
+            own, other = (main, tail) if p < 4 else (tail, main)
+            first = (base if p < 4 else 0) + 8 * gk
+            spread = lambda value, j: jnp.broadcast_to(value[:, j : j + 1], (8, 128))
+            pick = lambda value, i: jnp.broadcast_to(value[i : i + 1, :], (8, 128))
+            cols = {g: [spread(own[g], first + j) for j in range(8)] for g in range(gk, 4)}
+            low = {(i, j): pick(cols[gk][j], i) for j in range(8) for i in range(j, 8)}
+            own_rows = [pick(own[gk], i) for i in range(8)]
+            other_rows = [pick(other[gk], i) for i in range(8)]
+            inside = (lanes8 >= first) & (lanes8 < first + 8)
+            solved_rows = [
+                jnp.where(inside, jnp.where(lanes8 == first + i, 1.0, 0.0), own_rows[i])
+                for i in range(8)
+            ]
+            roots = []
+            for j in range(8):
+                root = lax.rsqrt(low[j, j])
+                inv = root * root
+                roots.append(root)
+                coef = {i: low[i, j] * inv for i in range(j + 1, 8)}
+                for i in range(j + 1, 8):
+                    for m in range(j + 1, i + 1):
+                        low[i, m] = low[i, m] - coef[i] * low[m, j]
+                    own_rows[i] = own_rows[i] - coef[i] * own_rows[j]
+                    solved_rows[i] = solved_rows[i] - coef[i] * solved_rows[j]
+                    other_rows[i] = other_rows[i] - coef[i] * other_rows[j]
+                for g in range(gk + 1, 4):
+                    for m in range(j + 1, 8):
+                        cols[g][m] = cols[g][m] - coef[m] * cols[g][j]
+                    factor_col = cols[g][j] * inv
+                    if j == 0:
+                        own[g] = jnp.where(inside, 0.0, own[g])
+                    own[g] = own[g] - factor_col * solved_rows[j]
+                    other[g] = other[g] - factor_col * other_rows[j]
+            new_own, new_other, new_scale = None, None, None
+            for i in range(8):
+                mixed = jnp.where(inside & (lanes8 > first + i), own_rows[i], solved_rows[i])
+                new_own = mixed if i == 0 else jnp.where(subs8 == i, mixed, new_own)
+                new_other = other_rows[i] if i == 0 else jnp.where(subs8 == i, other_rows[i], new_other)
+                new_scale = roots[i] if i == 0 else jnp.where(subs8 == i, roots[i], new_scale)
+            own[gk], other[gk], scale[gk] = new_own, new_other, new_scale
+        mainp = jnp.concatenate(main, axis=0)
+        tailp = jnp.concatenate(tail, axis=0)
+        scalep = jnp.concatenate(scale, axis=0)
+        if p < 4:
+            diag = lanes == rows + base
+            scaled = mainp * scalep
+            upper = jnp.where(lanes > rows + base, scaled, jnp.where(diag, 1.0 / scalep, 0.0))
+            full_main = jnp.where((lanes > rows + base) & (lanes < base + 32), 0.0, scaled)
+            side_out = tailp * scalep
+            factor_ref[base : base + 32, 0:128] = upper
+            factor_ref[base : base + 32, 128:160] = side_out[:, 0:32]
+            both = jnp.concatenate([upper, side_out], axis=1)
+            solved = jnp.concatenate([full_main, side_out], axis=1)
+            change = lax.dot_general(
+                both, solved, (((0,), (0,)), ((), ())),
+                precision=lax.Precision.HIGHEST, preferred_element_type=f32,
+            )
+            for q in range(p + 1, 5):
+                span = slice(32 * q, 32 * q + 32)
+                block = (lanes >= base) & (lanes < base + 32)
+                work[span, :] = jnp.where(block, 0.0, work[span, :]) - change[span, 0:128]
+                side[span, :] = side[span, :] - change[span, 128:256]
+        else:
+            diag = lanes == rows
+            factor_ref[128:160, 0:128] = jnp.zeros((32, 128), f32)
+            factor_ref[128:160, 128:160] = jnp.where(
+                lanes > rows, tailp * scalep, jnp.where(diag, 1.0 / scalep, 0.0)
+            )[:, 0:32]
+            left_ref[...] = (mainp * scalep).astype(jnp.bfloat16)
+            right_ref[...] = jnp.where(lanes <= rows, tailp * scalep, 0.0).astype(jnp.bfloat16)
+
+
+def factorize(packed):
+    return pl.pallas_call(
+        factor_kernel,
+        out_shape=(
+            jax.ShapeDtypeStruct((160, 160), jnp.float32),
+            jax.ShapeDtypeStruct((32, 128), jnp.bfloat16),
+            jax.ShapeDtypeStruct((32, 128), jnp.bfloat16),
+        ),
+        scratch_shapes=[pltpu.VMEM((160, 128), jnp.float32), pltpu.VMEM((160, 128), jnp.float32)],
+    )(packed)
+
+
+def pack(gram):
+    out = [[None] * 4 for _ in range(4)]
+    for (i, j), (r, c) in places.items():
+        out[r][c] = gram[32 * i : 32 * i + 32, 32 * j : 32 * j + 32]
+    return jnp.block([[b if b is not None else jnp.zeros((32, 32), jnp.float32) for b in row] for row in out])
+
+
+def summed(packed):
+    count_x, count_z = lax.axis_size("gx"), lax.axis_size("gz")
+    pieces = packed.reshape(count_x, -1, 128)
+    mine = lax.all_to_all(pieces, "gx", 0, 0).sum(0)
+    copies = jnp.broadcast_to(mine[None], (count_z,) + mine.shape)
+    mine = lax.all_to_all(copies, "gz", 0, 0).sum(0)
+    copies = jnp.broadcast_to(mine[None], (count_x,) + mine.shape)
+    return lax.all_to_all(copies, "gx", 0, 0).reshape(packed.shape)
 
 
 def body(velocity, spacing, basis, history, picks):
-    width_x = velocity.shape[1]
-    width_z = velocity.shape[2]
-    field = velocity
-    previous = jnp.zeros_like(velocity)
+    reach = 6
+    field = extended(velocity, (("gx", 1), ("gz", 2)), reach)
+    previous = jnp.zeros_like(field)
     for section in range(3):
-        padded = extended(field, (("gx", 1), ("gz", 2)), 2)
+        length_x, length_z = field.shape[1] - 4, field.shape[2] - 4
+        center = field[:, 2 : 2 + length_x, 2 : 2 + length_z]
+        before = previous[:, 2 : 2 + length_x, 2 : 2 + length_z]
         along_x = tuple(
-            (padded[:, start : start + width_x, 2 : 2 + width_z] for start in (0, 1, 3, 4))
+            (field[:, start : start + length_x, 2 : 2 + length_z] for start in (0, 1, 3, 4))
         )
         along_z = tuple(
-            (padded[:, 2 : 2 + width_x, start : start + width_z] for start in (0, 1, 3, 4))
+            (field[:, 2 : 2 + length_x, start : start + length_z] for start in (0, 1, 3, 4))
         )
-        current = tendency(field, along_x, along_z, spacing)
-        field = field + step_size * (gammas[section] * current + zetas[section] * previous)
+        current = tendency(center, along_x, along_z, spacing)
+        field = center + step_size * (gammas[section] * current + zetas[section] * before)
         previous = current
     fresh = field.astype(jnp.bfloat16)
     rank = basis.shape[0]
@@ -132,12 +231,9 @@
     )
     select = (indices[:, None] == jnp.arange(total, dtype=jnp.int32)[None, :]).astype(jnp.float32)
     local = exact_dot(exact_dot(select, full), select.T)
-    gram = lax.psum(local, ("gx", "gz")) / rows
-    factor = upper_factor(gram)
-    inverse = upper_inverse(factor)
-    rounded = inverse.astype(jnp.bfloat16)
-    part_basis = rounded[:rank, rank:]
-    part_snap = rounded[rank:, rank:]
+    factor, left, right = factorize(summed(pack(local)) / rows)
+    part_basis = left.T
+    part_snap = right[:, :snaps].T
     placing = (picks[:, None] == jnp.arange(stored, dtype=jnp.int32)[None, :]).astype(jnp.float32)
     stored_coef = exact_dot(placing.T, part_snap[:-1].astype(jnp.float32)).astype(jnp.bfloat16)
     fresh_coef = part_snap[-1:]

time: 867 us -> 103 us (0.12)
  waiting for transfers between devices: 257 us -> 4.67 us
  local copies, waits for them, and re-layouts: 213 us -> 13.2 us
  other arithmetic: 142 us -> 4.36 us
  loops' own time: 128 us -> 0 us
  matrix products: 88.2 us -> 22.9 us
  blocking collectives: 0 us -> 37.7 us
  between operations: 14.3 us -> 0.92 us
  starting transfers between devices: 21.2 us -> 10.8 us
    psum x1 -> x0, waiting for transfers between devices: 239 us -> none  [body(): gram = lax.psum(local, ('gx', 'gz')) / rows]
    dynamic_slice x480 -> x0, local copies, waits for them, and re-layouts: 200 us -> none  [the longest x160 96.6 us: row_step(): diag_value = lax.dynamic_slice_in_dim(lower_row, index, 1, 0)[0]]
    another operation x2 -> x0, loops' own time: 128 us -> none  [the longest x1 121 us: upper_factor(): lax.fori_loop(0, order, column_step, jnp.zeros((order, order), jnp.float32))]
    div x161 -> x1, other arithmetic: 105 us -> 0.64 us  [body(): factor, left, right = factorize(summed(pack(local)) / rows)]
    dot_general x323 -> x3, matrix products: 60.4 us -> 0.88 us  [exact_dot(): return jnp.dot(left, right, precision=lax.Precision.HIGHEST)]
    all_to_all x0 -> x3, blocking collectives: none -> 37.7 us  [the longest x1 16.7 us: summed(): mine = lax.all_to_all(copies, 'gz', 0, 0).sum(0)]
    add x322 -> x2, other arithmetic: 31.2 us -> 1.46 us  [body(): center + step_size * (gammas[section] * current + zetas[section] * before)]
  transfers between devices with their start and end apart: 13 -> 4, of which waited for: 10 -> 1; matrix products, arithmetic and copies ran while one was open for 3% -> 20% of each run, Pallas kernels for 0% -> 0%
where the time goes in v1:
time: 103 us
  blocking collectives  37.7 us (37%)
  matrix products  22.9 us (22%)
  local copies, waits for them, and re-layouts  13.2 us (13%)
  starting transfers between devices  10.8 us (10%)
  Pallas kernels  7.88 us (8%)
  waiting for transfers between devices  4.67 us (5%)
  other arithmetic  4.36 us (4%)
    all_to_all x1, blocking collectives, summed(): mine = lax.all_to_all(copies, 'gz', 0, 0).sum(0)  16.7 us
    dot_general x5, matrix products, inner(): lax.dot_general(left, right, (((1,), (1,)), ((), ())), preferred_element_...  13.3 us
    unnamed x24, local copies, waits for them, and re-layouts  11 us
    all_to_all x1, blocking collectives, summed(): return lax.all_to_all(copies, 'gx', 0, 0).reshape(packed.shape)  10.9 us
    all_to_all x1, blocking collectives, summed(): mine = lax.all_to_all(pieces, 'gx', 0, 0).sum(0)  10.2 us
    ppermute x2, starting transfers between devices, extended(): after = lax.ppermute(first, axis, down)  9.65 us
    pallas_call x1, Pallas kernels, factorize(): pl.pallas_call(factor_kernel, out_shape=(jax.ShapeDtypeStruct((160, 160),...  7.88 us
    dot_general x1, matrix products, body(): jnp.dot(part_basis.T, basis_flat, preferred_element_type=jnp.float32)  7 us
  transfers between devices with their start and end apart: 4, of which 1 were waited for; matrix products, arithmetic and copies ran while one was open for 20% of the time, Pallas kernels for 0%

profile of v1, /device:TPU:1, one launch (start us, length us, event | category | flops | bytes accessed | tf_op | source)
XLA Modules:
  0.0 102.6 jit_solution(12621200967192589288)
XLA Ops:
  0.6 1.0 fusion.60
  1.6 3.3 %collective-permute-start.1 = (f32[3,6,8,128]{3,2,1,0:T(8,128)S(1)}, f32[3,6,8,128]{3,2,1,0:T(8,128)S(1)}, u32[]{:S(2)}, u32[]{:S(2)}) collective-permute-start(f32[3,6,8,128]{3,2,1,0:T(8,128)S(1)} %get-tuple-element.34), channel_id=1, source_target_pairs={{32,0},{64,32},{96,64},{128,96},{160,128},{192,160},{224,192},{0,2... | collective-permute-start | bytes 221192 | tf_op jit(solution)/shard_map/ppermute | solution.py:23
  4.9 4.6 %fusion.19 = f32[40,40]{0,1:T(8,128)S(1)} fusion(bf16[40,3,8,8,128]{4,3,2,1,0:T(8,128)(2,1)} %param.12), kind=kOutput, calls=%fused_computation.17 | convolution fusion | flops 78643200 | bytes 1972480 | tf_op jit(solution)/shard_map/dot_general | solution.py:52
  9.5 9.3 %copy.53 = bf16[128,3,8,8,128]{0,4,3,2,1:T(8,128)(2,1)} copy(bf16[128,3,8,8,128]{4,3,2,1,0:T(8,128)(2,1)} %param.11) | data formatting | bytes 12582912 | tf_op args[2]
  18.8 4.4 %fusion.16 = f32[128,40]{0,1:T(8,128)S(1)} fusion(bf16[128,3,8,8,128]{0,4,3,2,1:T(8,128)(2,1)} %copy.53, bf16[40,3,8,8,128]{4,3,2,1,0:T(8,128)(2,1)S(1)} %copy-done.1), kind=kOutput, calls=%fused_computation.16 | convolution fusion | flops 251658240 | bytes 8278016 | tf_op jit(solution)/shard_map/dot_general | solution.py:52
  23.2 0.2 copy-done
  23.4 1.9 %convolution_bitcast_fusion = f32[128,128]{0,1:T(8,128)S(1)} fusion(bf16[128,3,8,8,128]{0,4,3,2,1:T(8,128)(2,1)S(1)} %copy-done), kind=kOutput, calls=%fused_computation.15 | convolution fusion | flops 805306368 | bytes 6356992 | tf_op jit(solution)/shard_map/dot_general | solution.py:52
  25.6 1.2 %collective-permute-start.2 = (f32[3,20,6,128]{3,2,1,0:T(8,128)S(1)}, f32[3,20,6,128]{3,2,1,0:T(8,128)S(1)}, u32[]{:S(2)}, u32[]{:S(2)}) collective-permute-start(f32[3,20,6,128]{3,2,1,0:T(8,128)S(1)} %get-tuple-element.24), channel_id=1, source_target_pairs={{0,1},{1,2},{2,3},{3,4},{4,5},{5,6},{6,7},{7,8},{8,9},{9,10},{10,1... | collective-permute-start | bytes 552968 | tf_op jit(solution)/shard_map/ppermute | solution.py:22
  26.8 6.4 %collective-permute-start.3 = (f32[3,20,6,128]{3,2,1,0:T(8,128)S(1)}, f32[3,20,6,128]{3,2,1,0:T(8,128)S(1)}, u32[]{:S(2)}, u32[]{:S(2)}) collective-permute-start(f32[3,20,6,128]{3,2,1,0:T(8,128)S(1)} %get-tuple-element.25), channel_id=1, source_target_pairs={{1,0},{2,1},{3,2},{4,3},{5,4},{6,5},{7,6},{8,7},{9,8},{10,9},{11,1... | collective-permute-start | bytes 552968 | tf_op jit(solution)/shard_map/ppermute | solution.py:23
  33.3 4.7 %collective-permute-done.2 = f32[3,20,6,128]{3,2,1,0:T(8,128)S(1)} collective-permute-done((f32[3,20,6,128]{3,2,1,0:T(8,128)S(1)}, f32[3,20,6,128]{3,2,1,0:T(8,128)S(1)}, u32[]{:S(2)}, u32[]{:S(2)}) %collective-permute-start.2) | collective-permute-done | bytes 184352 | tf_op jit(solution)/shard_map/ppermute | solution.py:22
  37.9 0.1 pad_maximum_fusion
  38.2 0.8 multiply_add_fusion
  39.1 0.7 fusion.24
  39.8 0.2 convert_convert_fusion
  40.0 0.6 convert_bitcast_fusion
  40.6 1.3 %fusion.9 = f32[1,40,1,1,1]{1,0,4,3,2:T(1,128)S(1)} fusion(bf16[40,3,8,8,128]{4,3,2,1,0:T(8,128)(2,1)S(1)} %copy-done.1, bf16[3,8,8,128,1]{3,2,1,0,4:T(8,128)(2,1)S(1)} %get-tuple-element.32), kind=kOutput, calls=%fused_computation.10 | convolution fusion | flops 1966080 | bytes 2015392 | tf_op jit(solution)/shard_map/dot_general | solution.py:52
  41.9 1.0 fusion.50
  43.0 0.7 pad_maximum_fusion.1
  43.7 0.1 copy.49
  43.8 0.4 fusion.25
  44.2 0.3 fusion.39
  44.8 10.2 %all_to_all.15 = f32[8,16,128]{2,1,0:T(8,128)S(1)} all-to-all(f32[8,16,128]{2,1,0:T(8,128)S(1)} %bitcast.80), channel_id=1, replica_groups=mesh['gx'=8,'gz'=32] {'gx'}, dimensions={0} | all-to-all | bytes 131072 | tf_op jit(solution)/shard_map/all_to_all | solution.py:183
  55.1 16.7 %all_to_all.16 = f32[32,16,128]{2,1,0:T(8,128)S(1)} all-to-all(f32[32,16,128]{2,1,0:T(8,128)S(1)} %broadcast_in_dim.7), channel_id=1, replica_groups=mesh['gx'=8,'gz'=32] {'gz'}, dimensions={0} | all-to-all | bytes 524288 | tf_op jit(solution)/shard_map/all_to_all | solution.py:185
  71.8 10.9 %all_to_all.17 = f32[8,16,128]{2,1,0:T(8,128)S(1)} all-to-all(f32[8,16,128]{2,1,0:T(8,128)S(1)} %broadcast_in_dim.8), channel_id=1, replica_groups=mesh['gx'=8,'gz'=32] {'gx'}, dimensions={0} | all-to-all | bytes 131072 | tf_op jit(solution)/shard_map/all_to_all | solution.py:187
  82.7 0.6 broadcast_multiply_fusion
  83.3 7.9 %shard_map.112 = (f32[160,160]{1,0:T(8,128)}, bf16[32,128]{1,0:T(8,128)(2,1)}, bf16[32,128]{1,0:T(8,128)(2,1)}) custom-call(f32[128,128]{1,0:T(8,128)} %bitcast.81), custom_call_target="tpu_custom_call" | custom-call | tf_op jit(solution)/shard_map/pallas_call | solution.py:162
  91.2 0.7 slice_bitcast_fusion.3
  91.9 0.2 convert_reduce_fusion
  92.1 0.2 convolution_convert_fusion
  92.3 1.8 %fusion.4 = f32[32,24576]{1,0:T(8,128)S(1)} fusion(bf16[40,32]{0,1:T(8,128)(2,1)S(1)} %convolution_convert_fusion, bf16[5,8,192,128]{3,2,1,0:T(8,128)(2,1)S(1)} %bitcast.77), kind=kOutput, calls=%fused_computation.5 | convolution fusion | flops 62914560 | bytes 5114368 | tf_op jit(solution)/shard_map/dot_general | solution.py:241
  94.1 7.0 %fusion.13 = bf16[4,8,192,128]{3,1,2,0:T(8,128)(2,1)S(1)} fusion(f32[24576]{0:T(1024)S(1)} %bitcast.79, f32[32]{0:T(128)S(1)} %convert_reduce_fusion, f32[32,24576]{1,0:T(8,128)S(1)} %fusion.4, bf16[32,128]{1,0:T(8,128)(2,1)S(1)} %copy-done.4, bf16[16,8,192,128]{3,2,1,0:T(8,128)(2,1)} %bitcast.76), kind=kOutput, calls=%fused_computation.14 | convolution fusion | flops 204472320 | bytes 11116672 | tf_op jit(solution)/shard_map/dot_general | solution.py:240
  101.1 1.5 %copy.63 = bf16[4,8,192,128]{3,2,1,0:T(8,128)(2,1)} copy(bf16[4,8,192,128]{3,1,2,0:T(8,128)(2,1)S(1)} %fusion.13) | data formatting | bytes 3145728
  (49 shorter events, 0.9 us)
Async XLA Ops:
  1.6 23.9 %collective-permute-start.1 = (f32[3,6,8,128]{3,2,1,0:T(8,128)S(1)}, f32[3,6,8,128]{3,2,1,0:T(8,128)S(1)}, u32[]{:S(2)}, u32[]{:S(2)}) collective-permute-start(f32[3,6,8,128]{3,2,1,0:T(8,128)S(1)} %get-tuple-element.34), channel_id=1, source_target_pairs={{32,0},{64,32},{96,64},{128,96},{160,128},{192,160},{224,192},{0,2... | collective-permute-start | bytes 221192 | tf_op jit(solution)/shard_map/ppermute | solution.py:23
  4.9 20.6 %collective-permute-start = (f32[3,6,8,128]{3,2,1,0:T(8,128)S(1)}, f32[3,6,8,128]{3,2,1,0:T(8,128)S(1)}, u32[]{:S(2)}, u32[]{:S(2)}) collective-permute-start(f32[3,6,8,128]{3,2,1,0:T(8,128)S(1)} %get-tuple-element.35), channel_id=1, source_target_pairs={{0,32},{32,64},{64,96},{96,128},{128,160},{160,192},{192,224},{224... | collective-permute-start | bytes 221192 | tf_op jit(solution)/shard_map/ppermute | solution.py:22
  9.5 9.3 %copy-start.1 = (bf16[40,3,8,8,128]{4,3,2,1,0:T(8,128)(2,1)S(1)}, bf16[40,3,8,8,128]{4,3,2,1,0:T(8,128)(2,1)}, u32[]{:S(2)}) copy-start(bf16[40,3,8,8,128]{4,3,2,1,0:T(8,128)(2,1)} %param.12) | copy-start | bytes 5898244
  18.8 4.6 %copy-start = (bf16[128,3,8,8,128]{0,4,3,2,1:T(8,128)(2,1)S(1)}, bf16[128,3,8,8,128]{0,4,3,2,1:T(8,128)(2,1)}, u32[]{:S(2)}) copy-start(bf16[128,3,8,8,128]{0,4,3,2,1:T(8,128)(2,1)} %copy.53) | copy-start | bytes 18874372
  23.4 1.9 %copy-start.7 = (s32[31]{0:T(128)S(1)}, s32[31]{0:T(128)}, u32[]{:S(2)}) copy-start(s32[31]{0:T(128)} %param.13) | copy-start | bytes 376
  23.4 2.2 %copy-start.2 = (f32[3,8,8,128]{3,2,1,0:T(8,128)S(1)}, f32[3,8,8,128]{3,2,1,0:T(8,128)}, u32[]{:S(2)}) copy-start(f32[3,8,8,128]{3,2,1,0:T(8,128)} %param.9) | copy-start | bytes 294916
  23.4 9.8 %copy-start.6 = (f32[129]{0:T(256)S(1)}, f32[129]{0:T(256)}, u32[]{:S(2)}) copy-start(f32[129]{0:T(256)} %param.10) | copy-start | bytes 1552
  25.3 12.9 %copy-start.5 = (f32[3]{0:T(128)S(1)}, f32[3]{0:T(128)}, u32[]{:S(2)}) copy-start(f32[3]{0:T(128)} %constant.32.clone) | copy-start | bytes 40
  25.6 12.3 %collective-permute-start.2 = (f32[3,20,6,128]{3,2,1,0:T(8,128)S(1)}, f32[3,20,6,128]{3,2,1,0:T(8,128)S(1)}, u32[]{:S(2)}, u32[]{:S(2)}) collective-permute-start(f32[3,20,6,128]{3,2,1,0:T(8,128)S(1)} %get-tuple-element.24), channel_id=1, source_target_pairs={{0,1},{1,2},{2,3},{3,4},{4,5},{5,6},{6,7},{7,8},{8,9},{9,10},{10,1... | collective-permute-start | bytes 552968 | tf_op jit(solution)/shard_map/ppermute | solution.py:22
  26.8 11.1 %collective-permute-start.3 = (f32[3,20,6,128]{3,2,1,0:T(8,128)S(1)}, f32[3,20,6,128]{3,2,1,0:T(8,128)S(1)}, u32[]{:S(2)}, u32[]{:S(2)}) collective-permute-start(f32[3,20,6,128]{3,2,1,0:T(8,128)S(1)} %get-tuple-element.25), channel_id=1, source_target_pairs={{1,0},{2,1},{3,2},{4,3},{5,4},{6,5},{7,6},{8,7},{9,8},{10,9},{11,1... | collective-permute-start | bytes 552968 | tf_op jit(solution)/shard_map/ppermute | solution.py:23
  38.2 3.8 %slice-start = ((s8[6291456]{0:T(1024)(128)(4,1)}), s8[2097152]{0:T(1024)(128)(4,1)S(1)}, s32[]{:S(2)}) async-start(s8[6291456]{0:T(1024)(128)(4,1)} %bitcast.74), calls=%async_computation.3 | async-start | bytes 4194304
  39.1 2.9 %slice-start.1 = ((s8[6291456]{0:T(1024)(128)(4,1)}), s8[4194304]{0:T(1024)(128)(4,1)S(1)}, s32[]{:S(2)}) async-start(s8[6291456]{0:T(1024)(128)(4,1)} %bitcast.74), calls=%async_computation.4 | async-start | bytes 8388608
  40.0 3.0 %copy-start.3 = (f32[3,8,8,128]{3,2,1,0:T(8,128)}, f32[3,8,8,128]{3,2,1,0:T(8,128)S(1)}, u32[]{:S(2)}) copy-start(f32[3,8,8,128]{3,2,1,0:T(8,128)S(1)} %get-tuple-element.10) | copy-start | bytes 294916
  91.2 2.9 %copy-start.4 = (bf16[32,128]{1,0:T(8,128)(2,1)S(1)}, bf16[32,128]{1,0:T(8,128)(2,1)}, u32[]{:S(2)}) copy-start(bf16[32,128]{1,0:T(8,128)(2,1)} %get-tuple-element.7) | copy-start | bytes 24580

commit v2 on v1

v2 whole, which is shorter than its diff:
```python
import functools

import jax
import jax.numpy as jnp
from jax import lax
from jax.experimental import pallas as pl
from jax.experimental.pallas import tpu as pltpu
from jax.sharding import PartitionSpec as P

step_size = 0.1
viscosity = 0.05
forcing = 0.5
gammas = (8.0 / 15.0, 5.0 / 12.0, 3.0 / 4.0)
zetas = (0.0, -17.0 / 60.0, -5.0 / 12.0)


def neighbours(last, first, axis):
    count = lax.axis_size(axis)
    up = [(i, (i + 1) % count) for i in range(count)]
    down = [(j, i) for i, j in up]
    return lax.ppermute(last, axis, up), lax.ppermute(first, axis, down)


def edges_kernel(own_ref, behind_ref, ahead_ref, padded_ref, last_ref, first_ref):
    padded_ref[...] = own_ref[...]
    padded_ref[:, :, 0:6, :] = behind_ref[:, :, 2:8, :]
    padded_ref[:, :, 14:20, :] = ahead_ref[:, :, 0:6, :]
    for target, starts in ((last_ref, (2, 4, 6)), (first_ref, (4, 2, 0))):
        target[:, :, 0:8, :] = padded_ref[:, starts[0] : starts[0] + 2, 6:14, :]
        target[:, :, 8:20, :] = padded_ref[:, starts[1] : starts[1] + 2, 4:16, :]
        target[:, :, 20:36, :] = padded_ref[:, starts[2] : starts[2] + 2, 2:18, :]


def edges(velocity, behind, ahead):
    return pl.pallas_call(
        edges_kernel,
        in_specs=[whole, whole, whole],
        out_specs=(whole, whole, whole),
        out_shape=(
            jax.ShapeDtypeStruct((3, 8, 24, 128), jnp.float32),
            jax.ShapeDtypeStruct((3, 2, 36, 128), jnp.float32),
            jax.ShapeDtypeStruct((3, 2, 36, 128), jnp.float32),
        ),
        compiler_params=pltpu.CompilerParams(vmem_limit_bytes=8 * 2**20),
        cost_estimate=pl.CostEstimate(flops=0, bytes_accessed=40 * 10**6, transcendentals=0),
    )(velocity, behind, ahead)


def advance(spacing_ref, padded_ref, behind_ref, ahead_ref, field_ref, even, odd, tend):
    even[...] = jnp.zeros(even.shape, jnp.float32)
    odd[...] = jnp.zeros(odd.shape, jnp.float32)
    even[:, 6:14, :, :] = padded_ref[...]
    for source, starts in ((behind_ref, (0, 2, 4)), (ahead_ref, (18, 16, 14))):
        even[:, starts[0] : starts[0] + 2, 6:14, :] = source[:, :, 0:8, :]
        even[:, starts[1] : starts[1] + 2, 4:16, :] = source[:, :, 8:20, :]
        even[:, starts[2] : starts[2] + 2, 2:18, :] = source[:, :, 20:36, :]
    lower, upper = spacing_ref[:, 0:128], spacing_ref[:, 1:129]
    y = lax.broadcasted_iota(jnp.int32, (1, 128), 1)
    slope = 1.0 / (lower + upper)
    slope_up = jnp.where(y < 127, slope, 0.0)
    slope_down = jnp.where(y > 0, slope, 0.0)
    curve_up = 2.0 * slope_up / upper
    curve_down = 2.0 * slope_down / lower
    curve_own = 2.0 * slope * (1.0 / upper + 1.0 / lower) + 5.0

    for section in range(3):
        source = odd if section == 1 else even
        first, count = 2 + 2 * section, 16 - 4 * section
        start, length = (2, 16) if section < 2 else (6, 8)
        span = slice(start, start + length)

        @pl.loop(first, first + count)
        def _(x):
            speed = [source[c, x, span, :] for c in range(3)]
            for c in range(3):
                own = speed[c]
                west, east = source[c, x - 1, span, :], source[c, x + 1, span, :]
                west_far, east_far = source[c, x - 2, span, :], source[c, x + 2, span, :]
                south = source[c, x, start - 1 : start - 1 + length, :]
                north = source[c, x, start + 1 : start + 1 + length, :]
                south_far = source[c, x, start - 2 : start - 2 + length, :]
                north_far = source[c, x, start + 2 : start + 2 + length, :]
                beneath = pltpu.roll(own, 1, 1)
                overhead = pltpu.roll(own, 127, 1)
                grad_x = (8.0 * (east - west) - (east_far - west_far)) * (1.0 / 12.0)
                grad_z = (8.0 * (north - south) - (north_far - south_far)) * (1.0 / 12.0)
                grad_y = overhead * slope_up - beneath * slope_down
                near = (east + west) + (north + south)
                far = (east_far + west_far) + (north_far + south_far)
                curve = (16.0 * near - far) * (1.0 / 12.0)
                curve = curve + overhead * curve_up + beneath * curve_down - own * curve_own
                advect = speed[0] * grad_x + speed[1] * grad_y + speed[2] * grad_z
                rate = viscosity * curve - advect
                if c == 0:
                    rate = rate + forcing
                change = gammas[section] * rate
                if section == 1:
                    change = change + zetas[1] * tend[c, x]
                if section == 2:
                    change = change + zetas[2] * tend[c, x, 4:12, :]
                result = own + step_size * change
                if section < 2:
                    tend[c, x] = rate
                    (even if section == 1 else odd)[c, x, span, :] = result
                else:
                    field_ref[pl.ds(pl.multiple_of((c * 8 + x - 6) * 8, 8), 8), :] = result


places = {(i, j): (i, j) for i in range(4) for j in range(i, 4)}
places.update({(4, 4): (1, 0), (2, 4): (2, 0), (3, 4): (2, 1), (0, 4): (3, 0), (1, 4): (3, 1)})
contract_last = (((1,), (1,)), ((), ()))
whole = pl.BlockSpec(memory_space=pltpu.VMEM)


def load_kernel(basis_ref, stored_ref, modes, snaps, sems):
    copies = []
    for chunk in range(6):
        span = pl.ds(32 * chunk, 32)
        copies += [
            pltpu.make_async_copy(basis_ref.at[:, span, :], modes.at[chunk], sems.at[0, chunk]),
            pltpu.make_async_copy(stored_ref.at[:, span, :], snaps.at[chunk], sems.at[1, chunk]),
        ]
    for copy in copies:
        copy.start()
    for copy in copies:
        copy.wait()


def loaded_parts(basis, stored):
    return pl.pallas_call(
        load_kernel,
        in_specs=[pl.BlockSpec(memory_space=pl.ANY)] * 2,
        out_specs=(whole, whole),
        out_shape=(
            jax.ShapeDtypeStruct((6, 128, 32, 128), jnp.bfloat16),
            jax.ShapeDtypeStruct((6, 40, 32, 128), jnp.bfloat16),
        ),
        scratch_shapes=[pltpu.SemaphoreType.DMA((2, 6))],
        compiler_params=pltpu.CompilerParams(vmem_limit_bytes=42 * 2**20),
        cost_estimate=pl.CostEstimate(flops=0, bytes_accessed=16 * 10**6, transcendentals=0),
    )(basis, stored)


def gram_kernel(
    picks_ref, basis_ref, stored_ref, spacing_ref, padded_ref, behind_ref, ahead_ref,
    packed_ref, turned_ref, fresh_ref, even, odd, tend,
):
    f32, bf16 = jnp.float32, jnp.bfloat16
    advance(spacing_ref, padded_ref, behind_ref, ahead_ref, fresh_ref, even, odd, tend)

    def step(chunk, total):
        for group in range(10):
            for half in range(2):
                rows = slice(16 * half, 16 * half + 16)
                place = pl.ds(pl.multiple_of(32 * chunk + 16 * half, 16), 16)
                if group < 8:
                    tile = basis_ref[chunk, 16 * group : 16 * group + 16, rows, :]
                else:
                    first = 16 * (group - 8)
                    tile = jnp.stack(
                        [
                            stored_ref[chunk, picks_ref[first + j], rows, :]
                            if first + j < 31
                            else fresh_ref[place, :].astype(bf16)
                            for j in range(16)
                        ],
                        axis=0,
                    )
                tile = jnp.swapaxes(tile, 0, 1)
                for s in range(16):
                    lanes = slice(256 * s + 128 * half, 256 * s + 128 * half + 128)
                    turned_ref[chunk, 16 * group : 16 * group + 16, lanes] = tile[s]
        block = turned_ref[chunk]
        return total + lax.dot_general(block, block, contract_last, preferred_element_type=f32)

    total = lax.fori_loop(0, 6, step, jnp.zeros((160, 160), f32))
    lanes = lax.broadcasted_iota(jnp.int32, (32, 128), 1)
    right = jnp.concatenate([total[:, 128:160], jnp.zeros((160, 96), f32)], axis=1)
    parts = [jnp.where(lanes >= 32 * p, total[32 * p : 32 * p + 32, 0:128], 0.0) for p in range(4)]
    for p in range(5):
        r, c = places[(p, 4)]
        part = right[32 * p : 32 * p + 32, :]
        parts[r] = parts[r] + (pltpu.roll(part, 32 * c, 1) if c else part)
    for r in range(16):
        packed_ref[:, 128 * r : 128 * r + 128] = parts[r // 4][8 * (r % 4) : 8 * (r % 4) + 8, :]


def local_gram(picks, *operands):
    return pl.pallas_call(
        gram_kernel,
        in_specs=[pl.BlockSpec(memory_space=pltpu.SMEM)] + [whole] * 6,
        out_specs=(whole, whole, whole),
        out_shape=(
            jax.ShapeDtypeStruct((8, 2048), jnp.float32),
            jax.ShapeDtypeStruct((6, 160, 4096), jnp.bfloat16),
            jax.ShapeDtypeStruct((192, 128), jnp.float32),
        ),
        scratch_shapes=[
            pltpu.VMEM((3, 20, 24, 128), jnp.float32),
            pltpu.VMEM((3, 20, 24, 128), jnp.float32),
            pltpu.VMEM((3, 20, 16, 128), jnp.float32),
        ],
        compiler_params=pltpu.CompilerParams(vmem_limit_bytes=16 * 2**20),
        cost_estimate=pl.CostEstimate(flops=2 * 10**9, bytes_accessed=16 * 10**6, transcendentals=0),
    )(picks, *operands)


def factor_kernel(rows_total, sums_ref, factor_ref, left_ref, right_ref, work, side):
    f32 = jnp.float32
    lanes8 = lax.broadcasted_iota(jnp.int32, (8, 128), 1)
    subs8 = lax.broadcasted_iota(jnp.int32, (8, 128), 0)
    lanes = lax.broadcasted_iota(jnp.int32, (32, 128), 1)
    rows = lax.broadcasted_iota(jnp.int32, (32, 128), 0)
    def loaded(r):
        tiles = [
            jnp.concatenate([sums_ref[j, :, 128 * q : 128 * q + 128] for j in range(8)], axis=0)
            for q in range(4 * r, 4 * r + 4)
        ]
        return jnp.concatenate(tiles, axis=0) / rows_total

    gathered = [loaded(r) for r in range(4)]
    for p in range(4):
        work[32 * p : 32 * p + 32, :] = jnp.where(lanes >= 32 * p, gathered[p], 0.0)
        r, c = places[(p, 4)]
        last = pltpu.roll(gathered[r], 128 - 32 * c, 1) if c else gathered[r]
        side[32 * p : 32 * p + 32, :] = jnp.where(lanes < 32, last, 0.0)
    work[128:160, :] = jnp.zeros((32, 128), f32)
    last = gathered[places[(4, 4)][0]]
    side[128:160, :] = jnp.where(lanes < 32, last, 0.0)

    for p in range(5):
        base = 32 * p
        main = [work[base + 8 * g : base + 8 * g + 8, :] for g in range(4)]
        tail = [side[base + 8 * g : base + 8 * g + 8, :] for g in range(4)]
        scale = [None] * 4
        for gk in range(4):
            own, other = (main, tail) if p < 4 else (tail, main)
            first = (base if p < 4 else 0) + 8 * gk
            spread = lambda value, j: jnp.broadcast_to(value[:, j : j + 1], (8, 128))
            pick = lambda value, i: jnp.broadcast_to(value[i : i + 1, :], (8, 128))
            cols = {g: [spread(own[g], first + j) for j in range(8)] for g in range(gk, 4)}
            low = {(i, j): pick(cols[gk][j], i) for j in range(8) for i in range(j, 8)}
            own_rows = [pick(own[gk], i) for i in range(8)]
            other_rows = [pick(other[gk], i) for i in range(8)]
            inside = (lanes8 >= first) & (lanes8 < first + 8)
            solved_rows = [
                jnp.where(inside, jnp.where(lanes8 == first + i, 1.0, 0.0), own_rows[i])
                for i in range(8)
            ]
            roots = []
            for j in range(8):
                root = lax.rsqrt(low[j, j])
                inv = root * root
                roots.append(root)
                coef = {i: low[i, j] * inv for i in range(j + 1, 8)}
                for i in range(j + 1, 8):
                    for m in range(j + 1, i + 1):
                        low[i, m] = low[i, m] - coef[i] * low[m, j]
                    own_rows[i] = own_rows[i] - coef[i] * own_rows[j]
                    solved_rows[i] = solved_rows[i] - coef[i] * solved_rows[j]
                    other_rows[i] = other_rows[i] - coef[i] * other_rows[j]
                for g in range(gk + 1, 4):
                    for m in range(j + 1, 8):
                        cols[g][m] = cols[g][m] - coef[m] * cols[g][j]
                    factor_col = cols[g][j] * inv
                    if j == 0:
                        own[g] = jnp.where(inside, 0.0, own[g])
                    own[g] = own[g] - factor_col * solved_rows[j]
                    other[g] = other[g] - factor_col * other_rows[j]
            new_own, new_other, new_scale = None, None, None
            for i in range(8):
                mixed = jnp.where(inside & (lanes8 > first + i), own_rows[i], solved_rows[i])
                new_own = mixed if i == 0 else jnp.where(subs8 == i, mixed, new_own)
                new_other = other_rows[i] if i == 0 else jnp.where(subs8 == i, other_rows[i], new_other)
                new_scale = roots[i] if i == 0 else jnp.where(subs8 == i, roots[i], new_scale)
            own[gk], other[gk], scale[gk] = new_own, new_other, new_scale
        mainp = jnp.concatenate(main, axis=0)
        tailp = jnp.concatenate(tail, axis=0)
        scalep = jnp.concatenate(scale, axis=0)
        if p < 4:
            diag = lanes == rows + base
            scaled = mainp * scalep
            upper = jnp.where(lanes > rows + base, scaled, jnp.where(diag, 1.0 / scalep, 0.0))
            full_main = jnp.where((lanes > rows + base) & (lanes < base + 32), 0.0, scaled)
            side_out = tailp * scalep
            factor_ref[base : base + 32, 0:128] = upper
            factor_ref[base : base + 32, 128:160] = side_out[:, 0:32]
            both = jnp.concatenate([upper, side_out], axis=1)
            solved = jnp.concatenate([full_main, side_out], axis=1)
            change = lax.dot_general(
                both, solved, (((0,), (0,)), ((), ())),
                precision=lax.Precision.HIGHEST, preferred_element_type=f32,
            )
            for q in range(p + 1, 5):
                span = slice(32 * q, 32 * q + 32)
                block = (lanes >= base) & (lanes < base + 32)
                work[span, :] = jnp.where(block, 0.0, work[span, :]) - change[span, 0:128]
                side[span, :] = side[span, :] - change[span, 128:256]
        else:
            diag = lanes == rows
            factor_ref[128:160, 0:128] = jnp.zeros((32, 128), f32)
            factor_ref[128:160, 128:160] = jnp.where(
                lanes > rows, tailp * scalep, jnp.where(diag, 1.0 / scalep, 0.0)
            )[:, 0:32]
            left_ref[...] = (mainp * scalep).astype(jnp.bfloat16)
            right_ref[...] = jnp.where(lanes <= rows, tailp * scalep, 0.0).astype(jnp.bfloat16)


def spread(left_ref, right_ref, turned_ref, out_ref, result, sems):
    f32, bf16 = jnp.float32, jnp.bfloat16
    coef = jnp.concatenate([left_ref[...], right_ref[:, 0:32]], axis=1)

    def copy(chunk):
        span = pl.ds(pl.multiple_of(32 * chunk, 32), 32)
        return pltpu.make_async_copy(result.at[chunk], out_ref.at[:, span, :], sems.at[chunk])

    @pl.loop(0, 6)
    def _(chunk):
        total = jnp.dot(coef, turned_ref[chunk], preferred_element_type=f32).astype(bf16)
        for group in range(2):
            for half in range(2):
                tile = jnp.stack(
                    [
                        total[16 * group : 16 * group + 16, 256 * s + 128 * half : 256 * s + 128 * half + 128]
                        for s in range(16)
                    ],
                    axis=0,
                )
                result[chunk, 16 * group : 16 * group + 16, 16 * half : 16 * half + 16, :] = jnp.swapaxes(tile, 0, 1)
        copy(chunk).start()

    @pl.loop(0, 6)
    def _(chunk):
        copy(chunk).wait()


def last_kernel(
    rows_total, sums_ref, turned_ref, factor_ref, out_ref, work, side, left, right, result, sems
):
    factor_kernel(rows_total, sums_ref, factor_ref, left, right, work, side)
    spread(left, right, turned_ref, out_ref, result, sems)


def finish(sums, turned, rows_total):
    return pl.pallas_call(
        functools.partial(last_kernel, rows_total),
        in_specs=[whole, whole],
        out_specs=(whole, pl.BlockSpec(memory_space=pl.ANY)),
        out_shape=(
            jax.ShapeDtypeStruct((160, 160), jnp.float32),
            jax.ShapeDtypeStruct((32, 192, 128), jnp.bfloat16),
        ),
        scratch_shapes=[
            pltpu.VMEM((160, 128), jnp.float32),
            pltpu.VMEM((160, 128), jnp.float32),
            pltpu.VMEM((32, 128), jnp.bfloat16),
            pltpu.VMEM((32, 128), jnp.bfloat16),
            pltpu.VMEM((6, 32, 32, 128), jnp.bfloat16),
            pltpu.SemaphoreType.DMA((6,)),
        ],
        compiler_params=pltpu.CompilerParams(vmem_limit_bytes=16 * 2**20),
    )(sums, turned)


def everyone(value, axis):
    count = lax.axis_size(axis)
    copies = jnp.broadcast_to(value.reshape(1, 1, -1), (count, 1, value.size))
    return lax.all_to_all(copies, axis, 0, 0)


def added(pieces):
    return functools.reduce(jnp.add, [pieces[i] for i in range(pieces.shape[0])])


def body(velocity, spacing, basis, history, picks):
    modes, stored = basis.shape[0], history.shape[0]
    rows_total = float(velocity.size * lax.axis_size("gx") * lax.axis_size("gz"))
    behind, ahead = neighbours(velocity, velocity[:, :, 0:6], "gz")
    own = jnp.pad(velocity, ((0, 0), (0, 0), (6, 10), (0, 0)))
    padded, last, first = edges(own, behind, ahead)
    behind, ahead = neighbours(last, first, "gx")
    packed, turned, field = local_gram(
        picks,
        *loaded_parts(basis.reshape(modes, -1, 128), history.reshape(stored, -1, 128)),
        spacing.reshape(1, -1),
        padded,
        behind,
        ahead,
    )
    mine = added(lax.all_to_all(packed.reshape(8, 1, -1), "gx", 0, 0))
    mine = added(everyone(mine, "gz"))
    factor, directions = finish(everyone(mine, "gx"), turned, rows_total)
    return (field.reshape(velocity.shape), factor, directions.reshape((32,) + velocity.shape))


def solution(mesh):
    return jax.shard_map(
        body,
        mesh=mesh,
        in_specs=(
            P(None, "gx", "gz", None),
            P(),
            P(None, None, "gx", "gz", None),
            P(None, None, "gx", "gz", None),
            P(),
        ),
        out_specs=(P(None, "gx", "gz", None), P(), P(None, None, "gx", "gz", None)),
        check_vma=False,
    )
```

time: 103 us -> 76.7 us (0.74)
  matrix products: 22.9 us -> 0 us
  Pallas kernels: 7.88 us -> 23.3 us
  local copies, waits for them, and re-layouts: 13.2 us -> 2.74 us
  other arithmetic: 4.36 us -> 0.14 us
  waiting for transfers between devices: 4.67 us -> 1.7 us
  blocking collectives: 37.7 us -> 36.6 us
    dot_general x10 -> x0, matrix products: 22.9 us -> none  [the longest x5 13.3 us: inner(): lax.dot_general(left, right, (((1,), (1,)), ((), ())), preferred_element_...]
    pallas_call x1 -> x4, Pallas kernels: 7.88 us -> 23.3 us  [the longest x1 10.3 us: finish(): pl.pallas_call(functools.partial(last_kernel, rows_total), in_specs=[whol...]
    unnamed x24 -> x6, local copies, waits for them, and re-layouts: 11 us -> 1.55 us
    ppermute x4, waiting for transfers between devices: 4.67 us -> 1.7 us  [neighbours(): return (lax.ppermute(last, axis, up), lax.ppermute(first, axis, down))]
    add x4 -> x2, other arithmetic: 1.54 us -> 0.14 us  [added(): functools.reduce(jnp.add, [pieces[i] for i in range(pieces.shape[0])])]
    slice x9 -> x0, local copies, waits for them, and re-layouts: 1.31 us -> none  [the longest x1 0.98 us: extended(): first = lax.slice_in_dim(shard, 0, width, axis=dim)]
    all_to_all x3, blocking collectives: 37.7 us -> 36.6 us  [the longest x2 27 us: everyone(): return lax.all_to_all(copies, axis, 0, 0)]
  transfers between devices with their start and end apart: 4 -> 4, of which waited for: 1 -> 2; matrix products, arithmetic and copies ran while one was open for 20% -> 1% of each run, Pallas kernels for 0% -> 4%
where the time goes in v2:
time: 76.7 us; the launch traced here: 76.4 us
  blocking collectives  36.6 us (48%)
  Pallas kernels  23.3 us (30%)
  starting transfers between devices  11.2 us (15%)
  local copies, waits for them, and re-layouts  2.74 us (4%)
  waiting for transfers between devices  1.7 us (2%)
    all_to_all x2, blocking collectives, everyone(): return lax.all_to_all(copies, axis, 0, 0)  27 us
    ppermute x4, starting transfers between devices, neighbours(): return (lax.ppermute(last, axis, up), lax.ppermute(first, axis, down))  11.2 us
    pallas_call x1, Pallas kernels, finish(): pl.pallas_call(functools.partial(last_kernel, rows_total), in_specs=[whol...  10.3 us
    pallas_call x1, Pallas kernels, local_gram(): pl.pallas_call(gram_kernel, in_specs=[pl.BlockSpec(memory_space=pltpu.SME...  10 us
    all_to_all x1, blocking collectives, body(): mine = added(lax.all_to_all(packed.reshape(8, 1, -1), 'gx', 0, 0))  9.67 us
    pallas_call x1, Pallas kernels, loaded_parts(): pl.pallas_call(load_kernel, in_specs=[pl.BlockSpec(memory_space=pl.ANY)]...  2.98 us
    ppermute x4, waiting for transfers between devices, neighbours(): return (lax.ppermute(last, axis, up), lax.ppermute(first, axis, down))  1.7 us
    unnamed x6, local copies, waits for them, and re-layouts  1.55 us
  transfers between devices with their start and end apart: 4, of which 2 were waited for; matrix products, arithmetic and copies ran while one was open for 1% of the time, Pallas kernels for 4%

profile of v2, /device:TPU:1, one launch (start us, length us, event | category | flops | bytes accessed | tf_op | source)
XLA Modules:
  0.0 76.4 jit_solution(912740690313302887)
XLA Ops:
  0.6 0.0 copy-start.2
  0.6 0.0 copy-start.1
  0.7 2.5 %collective-permute-start = (f32[3,8,8,128]{3,2,1,0:T(8,128)}, f32[3,8,8,128]{3,2,1,0:T(8,128)S(1)}, u32[]{:S(2)}, u32[]{:S(2)}) collective-permute-start(f32[3,8,8,128]{3,2,1,0:T(8,128)} %param.5), channel_id=1, source_target_pairs={{0,1},{1,2},{2,3},{3,4},{4,5},{5,6},{6,7},{7,8},{8,9},{9,10},{10,1... | collective-permute-start | bytes 294920 | tf_op jit(solution)/shard_map/ppermute | solution.py:21
  3.2 6.2 %collective-permute-start.1 = (f32[3,8,6,128]{3,2,1,0:T(8,128)}, f32[3,8,6,128]{3,2,1,0:T(8,128)S(1)}, u32[]{:S(2)}, u32[]{:S(2)}) collective-permute-start(f32[3,8,6,128]{3,2,1,0:T(8,128)} %bitcast.13), channel_id=1, source_target_pairs={{1,0},{2,1},{3,2},{4,3},{5,4},{6,5},{7,6},{8,7},{9,8},{10,9},{11,1... | collective-permute-start | bytes 221192 | tf_op jit(solution)/shard_map/ppermute | solution.py:21
  9.4 0.9 %pad.4.own_ref = f32[3,8,24,128]{3,2,1,0:T(8,128)S(1)} pad(f32[3,8,8,128]{3,2,1,0:T(8,128)} %param.5, f32[]{:T(128)} %constant.2.clone.1), padding=0_0x0_0x6_10x0_0 | pad | bytes 393220 | tf_op jit(solution)/shard_map/jit(_pad)/pad | solution.py:379
  10.4 1.0 %collective-permute-done.1.ahead_ref = f32[3,8,6,128]{3,2,1,0:T(8,128)S(1)} collective-permute-done((f32[3,8,6,128]{3,2,1,0:T(8,128)}, f32[3,8,6,128]{3,2,1,0:T(8,128)S(1)}, u32[]{:S(2)}, u32[]{:S(2)}) %collective-permute-start.1) | collective-permute-done | bytes 73760 | tf_op jit(solution)/shard_map/ppermute | solution.py:21
  11.4 0.7 collective-permute-done.behind_ref
  12.1 0.1 shard_map.77
  12.1 2.4 %collective-permute-start.2 = (f32[3,2,36,128]{3,2,1,0:T(8,128)S(1)}, f32[3,2,36,128]{3,2,1,0:T(8,128)S(1)}, u32[]{:S(2)}, u32[]{:S(2)}) collective-permute-start(f32[3,2,36,128]{3,2,1,0:T(8,128)S(1)} %get-tuple-element.16), channel_id=1, source_target_pairs={{0,32},{32,64},{64,96},{96,128},{128,160},{160,192},{192,224},{224... | collective-permute-start | bytes 331784 | tf_op jit(solution)/shard_map/ppermute | solution.py:21
  14.5 0.0 collective-permute-start.3
  14.5 0.0 copy-start
  14.5 1.5 %copy-done = bf16[40,3,8,8,128]{4,3,2,1,0:T(8,128)(2,1)S(1)} copy-done((bf16[40,3,8,8,128]{4,3,2,1,0:T(8,128)(2,1)S(1)}, bf16[40,3,8,8,128]{4,3,2,1,0:T(8,128)(2,1)}, u32[]{:S(2)}) %copy-start) | copy-done | bytes 1966104
  16.1 3.0 %shard_map.76 = (bf16[6,128,32,128]{3,2,1,0:T(8,128)(2,1)S(1)}, bf16[6,40,32,128]{3,2,1,0:T(8,128)(2,1)S(1)}) custom-call(bf16[128,192,128]{2,1,0:T(8,128)(2,1)} %bitcast.12, bf16[40,192,128]{2,1,0:T(8,128)(2,1)S(1)} %bitcast.9), custom_call_target="tpu_custom_call" | custom-call | bytes 16000000 | tf_op jit(solution)/shard_map/pallas_call | solution.py:130
  19.1 0.0 collective-permute-done.2.behind_ref
  19.1 0.0 collective-permute-done.3.ahead_ref
  19.1 0.0 copy-done.2
  19.1 0.0 copy-done.1
  19.1 10.0 %shard_map.78 = (f32[8,2048]{1,0:T(8,128)S(1)}, bf16[6,160,4096]{2,1,0:T(8,128)(2,1)S(1)}, f32[192,128]{1,0:T(8,128)}) custom-call(s32[31]{0:T(128)S(1)} %copy-done.2, bf16[6,128,32,128]{3,2,1,0:T(8,128)(2,1)S(1)} %get-tuple-element.13.basis_ref, bf16[6,40,32,128]{3,2,1,0:T(8,128)(2,1)S(1)} %get-tuple-element.14.stored_ref, f32[1,129]{1,0:T(1,128)S(1)} %bitcast.11, ...), custom_call_target="tpu_custom_call" | custom-call | flops 2000000000 | bytes 16000000 | tf_op jit(solution)/shard_map/pallas_call | solution.py:189
  29.1 0.1 copy.8
  29.2 9.7 %all_to_all.15 = f32[8,1,2048]{2,1,0:T(1,128)S(1)} all-to-all(f32[8,1,2048]{2,1,0:T(1,128)S(1)} %copy.8), channel_id=1, replica_groups=mesh['gx'=8,'gz'=32] {'gx'}, dimensions={0} | all-to-all | bytes 131072 | tf_op jit(solution)/shard_map/all_to_all | solution.py:390
  38.9 0.1 broadcast_in_dim.15
  39.0 16.1 %all_to_all.16 = f32[32,1,2048]{2,1,0:T(1,128)S(1)} all-to-all(f32[32,1,2048]{2,1,0:T(1,128)S(1)} %broadcast_in_dim.15), channel_id=1, replica_groups=mesh['gx'=8,'gz'=32] {'gz'}, dimensions={0} | all-to-all | bytes 524288 | tf_op jit(solution)/shard_map/all_to_all | solution.py:368
  55.1 0.1 slice_add_fusion
  55.3 10.9 %all_to_all.17.sums_ref = f32[8,1,2048]{2,1,0:T(1,128)S(1)} all-to-all(f32[8,1,2048]{2,1,0:T(1,128)S(1)} %broadcast_in_dim.17), channel_id=1, replica_groups=mesh['gx'=8,'gz'=32] {'gx'}, dimensions={0} | all-to-all | bytes 131072 | tf_op jit(solution)/shard_map/all_to_all | solution.py:368
  66.2 10.3 %shard_map.79 = (f32[160,160]{1,0:T(8,128)}, bf16[32,192,128]{2,1,0:T(8,128)(2,1)}) custom-call(f32[8,1,2048]{2,1,0:T(1,128)S(1)} %all_to_all.17.sums_ref, bf16[6,160,4096]{2,1,0:T(8,128)(2,1)S(1)} %get-tuple-element.20.turned_ref), custom_call_target="tpu_custom_call" | custom-call | tf_op jit(solution)/shard_map/pallas_call | solution.py:345
  (2 shorter events, 0.1 us)
Async XLA Ops:
  0.6 18.5 %copy-start.2 = (s32[31]{0:T(128)S(1)}, s32[31]{0:T(128)}, u32[]{:S(2)}) copy-start(s32[31]{0:T(128)} %picks_ref.1) | copy-start | bytes 376
  0.6 18.5 %copy-start.1 = (f32[129]{0:T(256)S(1)}, f32[129]{0:T(256)}, u32[]{:S(2)}) copy-start(f32[129]{0:T(256)} %param.6) | copy-start | bytes 1552
  0.7 11.4 %collective-permute-start = (f32[3,8,8,128]{3,2,1,0:T(8,128)}, f32[3,8,8,128]{3,2,1,0:T(8,128)S(1)}, u32[]{:S(2)}, u32[]{:S(2)}) collective-permute-start(f32[3,8,8,128]{3,2,1,0:T(8,128)} %param.5), channel_id=1, source_target_pairs={{0,1},{1,2},{2,3},{3,4},{4,5},{5,6},{6,7},{7,8},{8,9},{9,10},{10,1... | collective-permute-start | bytes 294920 | tf_op jit(solution)/shard_map/ppermute | solution.py:21
  3.2 8.2 %collective-permute-start.1 = (f32[3,8,6,128]{3,2,1,0:T(8,128)}, f32[3,8,6,128]{3,2,1,0:T(8,128)S(1)}, u32[]{:S(2)}, u32[]{:S(2)}) collective-permute-start(f32[3,8,6,128]{3,2,1,0:T(8,128)} %bitcast.13), channel_id=1, source_target_pairs={{1,0},{2,1},{3,2},{4,3},{5,4},{6,5},{7,6},{8,7},{9,8},{10,9},{11,1... | collective-permute-start | bytes 221192 | tf_op jit(solution)/shard_map/ppermute | solution.py:21
  12.1 7.0 %collective-permute-start.2 = (f32[3,2,36,128]{3,2,1,0:T(8,128)S(1)}, f32[3,2,36,128]{3,2,1,0:T(8,128)S(1)}, u32[]{:S(2)}, u32[]{:S(2)}) collective-permute-start(f32[3,2,36,128]{3,2,1,0:T(8,128)S(1)} %get-tuple-element.16), channel_id=1, source_target_pairs={{0,32},{32,64},{64,96},{96,128},{128,160},{160,192},{192,224},{224... | collective-permute-start | bytes 331784 | tf_op jit(solution)/shard_map/ppermute | solution.py:21
  14.5 4.5 %collective-permute-start.3 = (f32[3,2,36,128]{3,2,1,0:T(8,128)S(1)}, f32[3,2,36,128]{3,2,1,0:T(8,128)S(1)}, u32[]{:S(2)}, u32[]{:S(2)}) collective-permute-start(f32[3,2,36,128]{3,2,1,0:T(8,128)S(1)} %get-tuple-element.17), channel_id=1, source_target_pairs={{32,0},{64,32},{96,64},{128,96},{160,128},{192,160},{224,192},{0,2... | collective-permute-start | bytes 331784 | tf_op jit(solution)/shard_map/ppermute | solution.py:21
  14.5 1.5 %copy-start = (bf16[40,3,8,8,128]{4,3,2,1,0:T(8,128)(2,1)S(1)}, bf16[40,3,8,8,128]{4,3,2,1,0:T(8,128)(2,1)}, u32[]{:S(2)}) copy-start(bf16[40,3,8,8,128]{4,3,2,1,0:T(8,128)(2,1)} %param.8) | copy-start | bytes 5898244

commit v3 on v2

--- a/solution.py
+++ b/solution.py
@@ -69,7 +69,7 @@
         start, length = (2, 16) if section < 2 else (6, 8)
         span = slice(start, start + length)
 
-        @pl.loop(first, first + count)
+        @pl.loop(first, first + count, unroll=4)
         def _(x):
             speed = [source[c, x, span, :] for c in range(3)]
             for c in range(3):
@@ -152,7 +152,7 @@
         for group in range(10):
             for half in range(2):
                 rows = slice(16 * half, 16 * half + 16)
-                place = pl.ds(pl.multiple_of(32 * chunk + 16 * half, 16), 16)
+                place = slice(32 * chunk + 16 * half, 32 * chunk + 16 * half + 16)
                 if group < 8:
                     tile = basis_ref[chunk, 16 * group : 16 * group + 16, rows, :]
                 else:
@@ -173,7 +173,9 @@
         block = turned_ref[chunk]
         return total + lax.dot_general(block, block, contract_last, preferred_element_type=f32)
 
-    total = lax.fori_loop(0, 6, step, jnp.zeros((160, 160), f32))
+    total = jnp.zeros((160, 160), f32)
+    for chunk in range(6):
+        total = step(chunk, total)
     lanes = lax.broadcasted_iota(jnp.int32, (32, 128), 1)
     right = jnp.concatenate([total[:, 128:160], jnp.zeros((160, 96), f32)], axis=1)
     parts = [jnp.where(lanes >= 32 * p, total[32 * p : 32 * p + 32, 0:128], 0.0) for p in range(4)]
@@ -287,15 +289,22 @@
             factor_ref[base : base + 32, 128:160] = side_out[:, 0:32]
             both = jnp.concatenate([upper, side_out], axis=1)
             solved = jnp.concatenate([full_main, side_out], axis=1)
-            change = lax.dot_general(
-                both, solved, (((0,), (0,)), ((), ())),
-                precision=lax.Precision.HIGHEST, preferred_element_type=f32,
-            )
-            for q in range(p + 1, 5):
-                span = slice(32 * q, 32 * q + 32)
-                block = (lanes >= base) & (lanes < base + 32)
-                work[span, :] = jnp.where(block, 0.0, work[span, :]) - change[span, 0:128]
-                side[span, :] = side[span, :] - change[span, 128:256]
+            block = (lanes >= base) & (lanes < base + 32)
+
+            def reduce_rows(start, stop):
+                change = lax.dot_general(
+                    both[:, start:stop], solved, (((0,), (0,)), ((), ())),
+                    precision=lax.Precision.HIGHEST, preferred_element_type=f32,
+                )
+                for q in range(start // 32, stop // 32):
+                    span = slice(32 * q, 32 * q + 32)
+                    part = change[32 * q - start : 32 * q - start + 32, :]
+                    work[span, :] = jnp.where(block, 0.0, work[span, :]) - part[:, 0:128]
+                    side[span, :] = side[span, :] - part[:, 128:256]
+
+            reduce_rows(base + 32, base + 64)
+            if p < 3:
+                reduce_rows(base + 64, 160)
         else:
             diag = lanes == rows
             factor_ref[128:160, 0:128] = jnp.zeros((32, 128), f32)
@@ -314,7 +323,7 @@
         span = pl.ds(pl.multiple_of(32 * chunk, 32), 32)
         return pltpu.make_async_copy(result.at[chunk], out_ref.at[:, span, :], sems.at[chunk])
 
-    @pl.loop(0, 6)
+    @pl.loop(0, 6, unroll=3)
     def _(chunk):
         total = jnp.dot(coef, turned_ref[chunk], preferred_element_type=f32).astype(bf16)
         for group in range(2):

time: 76.7 us -> 71.9 us (0.937)
  Pallas kernels: 23.3 us -> 18.5 us
    pallas_call x1, Pallas kernels: 10 us -> 6.79 us  [local_gram(): pl.pallas_call(gram_kernel, in_specs=[pl.BlockSpec(memory_space=pltpu.SME...]
    pallas_call x1, Pallas kernels: 10.3 us -> 8.73 us  [finish(): pl.pallas_call(functools.partial(last_kernel, rows_total), in_specs=[whol...]
where the time goes in v3:
time: 71.9 us; the launch traced here: 71.7 us
  blocking collectives  36.6 us (51%)
  Pallas kernels  18.5 us (26%)
  starting transfers between devices  11.2 us (16%)
  local copies, waits for them, and re-layouts  2.74 us (4%)
  waiting for transfers between devices  1.7 us (2%)
  between operations  0.73 us (1%)
    all_to_all x2, blocking collectives, everyone(): return lax.all_to_all(copies, axis, 0, 0)  27 us
    ppermute x4, starting transfers between devices, neighbours(): return (lax.ppermute(last, axis, up), lax.ppermute(first, axis, down))  11.2 us
    all_to_all x1, blocking collectives, body(): mine = added(lax.all_to_all(packed.reshape(8, 1, -1), 'gx', 0, 0))  9.68 us
    pallas_call x1, Pallas kernels, finish(): pl.pallas_call(functools.partial(last_kernel, rows_total), in_specs=[whol...  8.73 us
    pallas_call x1, Pallas kernels, local_gram(): pl.pallas_call(gram_kernel, in_specs=[pl.BlockSpec(memory_space=pltpu.SME...  6.79 us
    pallas_call x1, Pallas kernels, loaded_parts(): pl.pallas_call(load_kernel, in_specs=[pl.BlockSpec(memory_space=pl.ANY)]...  2.98 us
    ppermute x4, waiting for transfers between devices, neighbours(): return (lax.ppermute(last, axis, up), lax.ppermute(first, axis, down))  1.7 us
    unnamed x6, local copies, waits for them, and re-layouts  1.55 us
  transfers between devices with their start and end apart: 4, of which 2 were waited for; matrix products, arithmetic and copies ran while one was open for 1% of the time, Pallas kernels for 4%

profile of v3, /device:TPU:1, one launch (start us, length us, event | category | flops | bytes accessed | tf_op | source)
XLA Modules:
  0.0 71.7 jit_solution(16851342554798007497)
XLA Ops:
  0.6 0.0 copy-start.2
  0.6 0.0 copy-start.1
  0.7 2.5 %collective-permute-start = (f32[3,8,8,128]{3,2,1,0:T(8,128)}, f32[3,8,8,128]{3,2,1,0:T(8,128)S(1)}, u32[]{:S(2)}, u32[]{:S(2)}) collective-permute-start(f32[3,8,8,128]{3,2,1,0:T(8,128)} %param.5), channel_id=1, source_target_pairs={{0,1},{1,2},{2,3},{3,4},{4,5},{5,6},{6,7},{7,8},{8,9},{9,10},{10,1... | collective-permute-start | bytes 294920 | tf_op jit(solution)/shard_map/ppermute | solution.py:21
  3.2 6.2 %collective-permute-start.1 = (f32[3,8,6,128]{3,2,1,0:T(8,128)}, f32[3,8,6,128]{3,2,1,0:T(8,128)S(1)}, u32[]{:S(2)}, u32[]{:S(2)}) collective-permute-start(f32[3,8,6,128]{3,2,1,0:T(8,128)} %bitcast.13), channel_id=1, source_target_pairs={{1,0},{2,1},{3,2},{4,3},{5,4},{6,5},{7,6},{8,7},{9,8},{10,9},{11,1... | collective-permute-start | bytes 221192 | tf_op jit(solution)/shard_map/ppermute | solution.py:21
  9.4 0.9 %pad.4.own_ref = f32[3,8,24,128]{3,2,1,0:T(8,128)S(1)} pad(f32[3,8,8,128]{3,2,1,0:T(8,128)} %param.5, f32[]{:T(128)} %constant.2.clone.1), padding=0_0x0_0x6_10x0_0 | pad | bytes 393220 | tf_op jit(solution)/shard_map/jit(_pad)/pad | solution.py:388
  10.4 1.0 %collective-permute-done.1.ahead_ref = f32[3,8,6,128]{3,2,1,0:T(8,128)S(1)} collective-permute-done((f32[3,8,6,128]{3,2,1,0:T(8,128)}, f32[3,8,6,128]{3,2,1,0:T(8,128)S(1)}, u32[]{:S(2)}, u32[]{:S(2)}) %collective-permute-start.1) | collective-permute-done | bytes 73760 | tf_op jit(solution)/shard_map/ppermute | solution.py:21
  11.4 0.7 collective-permute-done.behind_ref
  12.1 0.1 shard_map.77
  12.1 2.4 %collective-permute-start.2 = (f32[3,2,36,128]{3,2,1,0:T(8,128)S(1)}, f32[3,2,36,128]{3,2,1,0:T(8,128)S(1)}, u32[]{:S(2)}, u32[]{:S(2)}) collective-permute-start(f32[3,2,36,128]{3,2,1,0:T(8,128)S(1)} %get-tuple-element.16), channel_id=1, source_target_pairs={{0,32},{32,64},{64,96},{96,128},{128,160},{160,192},{192,224},{224... | collective-permute-start | bytes 331784 | tf_op jit(solution)/shard_map/ppermute | solution.py:21
  14.5 0.0 collective-permute-start.3
  14.5 0.0 copy-start
  14.5 1.5 %copy-done = bf16[40,3,8,8,128]{4,3,2,1,0:T(8,128)(2,1)S(1)} copy-done((bf16[40,3,8,8,128]{4,3,2,1,0:T(8,128)(2,1)S(1)}, bf16[40,3,8,8,128]{4,3,2,1,0:T(8,128)(2,1)}, u32[]{:S(2)}) %copy-start) | copy-done | bytes 1966104
  16.1 3.0 %shard_map.76 = (bf16[6,128,32,128]{3,2,1,0:T(8,128)(2,1)S(1)}, bf16[6,40,32,128]{3,2,1,0:T(8,128)(2,1)S(1)}) custom-call(bf16[128,192,128]{2,1,0:T(8,128)(2,1)} %bitcast.12, bf16[40,192,128]{2,1,0:T(8,128)(2,1)S(1)} %bitcast.9), custom_call_target="tpu_custom_call" | custom-call | bytes 16000000 | tf_op jit(solution)/shard_map/pallas_call | solution.py:130
  19.1 0.0 collective-permute-done.2.behind_ref
  19.1 0.0 collective-permute-done.3.ahead_ref
  19.1 0.0 copy-done.2
  19.1 0.0 copy-done.1
  19.1 6.8 %shard_map.78 = (f32[8,2048]{1,0:T(8,128)S(1)}, bf16[6,160,4096]{2,1,0:T(8,128)(2,1)S(1)}, f32[192,128]{1,0:T(8,128)}) custom-call(s32[31]{0:T(128)S(1)} %copy-done.2, bf16[6,128,32,128]{3,2,1,0:T(8,128)(2,1)S(1)} %get-tuple-element.13.basis_ref, bf16[6,40,32,128]{3,2,1,0:T(8,128)(2,1)S(1)} %get-tuple-element.14.stored_ref, f32[1,129]{1,0:T(1,128)S(1)} %bitcast.11, ...), custom_call_target="tpu_custom_call" | custom-call | flops 2000000000 | bytes 16000000 | tf_op jit(solution)/shard_map/pallas_call | solution.py:191
  25.9 0.1 copy.8
  26.0 9.7 %all_to_all.15 = f32[8,1,2048]{2,1,0:T(1,128)S(1)} all-to-all(f32[8,1,2048]{2,1,0:T(1,128)S(1)} %copy.8), channel_id=1, replica_groups=mesh['gx'=8,'gz'=32] {'gx'}, dimensions={0} | all-to-all | bytes 131072 | tf_op jit(solution)/shard_map/all_to_all | solution.py:399
  35.7 0.1 broadcast_in_dim.15
  35.8 16.1 %all_to_all.16 = f32[32,1,2048]{2,1,0:T(1,128)S(1)} all-to-all(f32[32,1,2048]{2,1,0:T(1,128)S(1)} %broadcast_in_dim.15), channel_id=1, replica_groups=mesh['gx'=8,'gz'=32] {'gz'}, dimensions={0} | all-to-all | bytes 524288 | tf_op jit(solution)/shard_map/all_to_all | solution.py:377
  51.9 0.1 slice_add_fusion
  52.1 10.9 %all_to_all.17.sums_ref = f32[8,1,2048]{2,1,0:T(1,128)S(1)} all-to-all(f32[8,1,2048]{2,1,0:T(1,128)S(1)} %broadcast_in_dim.17), channel_id=1, replica_groups=mesh['gx'=8,'gz'=32] {'gx'}, dimensions={0} | all-to-all | bytes 131072 | tf_op jit(solution)/shard_map/all_to_all | solution.py:377
  63.0 8.7 %shard_map.79 = (f32[160,160]{1,0:T(8,128)}, bf16[32,192,128]{2,1,0:T(8,128)(2,1)}) custom-call(f32[8,1,2048]{2,1,0:T(1,128)S(1)} %all_to_all.17.sums_ref, bf16[6,160,4096]{2,1,0:T(8,128)(2,1)S(1)} %get-tuple-element.20.turned_ref), custom_call_target="tpu_custom_call" | custom-call | tf_op jit(solution)/shard_map/pallas_call | solution.py:354
  (2 shorter events, 0.1 us)
Async XLA Ops:
  0.6 18.5 %copy-start.2 = (s32[31]{0:T(128)S(1)}, s32[31]{0:T(128)}, u32[]{:S(2)}) copy-start(s32[31]{0:T(128)} %picks_ref.1) | copy-start | bytes 376
  0.6 18.5 %copy-start.1 = (f32[129]{0:T(256)S(1)}, f32[129]{0:T(256)}, u32[]{:S(2)}) copy-start(f32[129]{0:T(256)} %param.6) | copy-start | bytes 1552
  0.7 11.4 %collective-permute-start = (f32[3,8,8,128]{3,2,1,0:T(8,128)}, f32[3,8,8,128]{3,2,1,0:T(8,128)S(1)}, u32[]{:S(2)}, u32[]{:S(2)}) collective-permute-start(f32[3,8,8,128]{3,2,1,0:T(8,128)} %param.5), channel_id=1, source_target_pairs={{0,1},{1,2},{2,3},{3,4},{4,5},{5,6},{6,7},{7,8},{8,9},{9,10},{10,1... | collective-permute-start | bytes 294920 | tf_op jit(solution)/shard_map/ppermute | solution.py:21
  3.2 8.2 %collective-permute-start.1 = (f32[3,8,6,128]{3,2,1,0:T(8,128)}, f32[3,8,6,128]{3,2,1,0:T(8,128)S(1)}, u32[]{:S(2)}, u32[]{:S(2)}) collective-permute-start(f32[3,8,6,128]{3,2,1,0:T(8,128)} %bitcast.13), channel_id=1, source_target_pairs={{1,0},{2,1},{3,2},{4,3},{5,4},{6,5},{7,6},{8,7},{9,8},{10,9},{11,1... | collective-permute-start | bytes 221192 | tf_op jit(solution)/shard_map/ppermute | solution.py:21
  12.1 7.0 %collective-permute-start.2 = (f32[3,2,36,128]{3,2,1,0:T(8,128)S(1)}, f32[3,2,36,128]{3,2,1,0:T(8,128)S(1)}, u32[]{:S(2)}, u32[]{:S(2)}) collective-permute-start(f32[3,2,36,128]{3,2,1,0:T(8,128)S(1)} %get-tuple-element.16), channel_id=1, source_target_pairs={{0,32},{32,64},{64,96},{96,128},{128,160},{160,192},{192,224},{224... | collective-permute-start | bytes 331784 | tf_op jit(solution)/shard_map/ppermute | solution.py:21
  14.5 4.5 %collective-permute-start.3 = (f32[3,2,36,128]{3,2,1,0:T(8,128)S(1)}, f32[3,2,36,128]{3,2,1,0:T(8,128)S(1)}, u32[]{:S(2)}, u32[]{:S(2)}) collective-permute-start(f32[3,2,36,128]{3,2,1,0:T(8,128)S(1)} %get-tuple-element.17), channel_id=1, source_target_pairs={{32,0},{64,32},{96,64},{128,96},{160,128},{192,160},{224,192},{0,2... | collective-permute-start | bytes 331784 | tf_op jit(solution)/shard_map/ppermute | solution.py:21
  14.5 1.5 %copy-start = (bf16[40,3,8,8,128]{4,3,2,1,0:T(8,128)(2,1)S(1)}, bf16[40,3,8,8,128]{4,3,2,1,0:T(8,128)(2,1)}, u32[]{:S(2)}) copy-start(bf16[40,3,8,8,128]{4,3,2,1,0:T(8,128)(2,1)} %param.8) | copy-start | bytes 5898244

commit v4 on v3

--- a/solution.py
+++ b/solution.py
@@ -149,8 +149,8 @@
     advance(spacing_ref, padded_ref, behind_ref, ahead_ref, fresh_ref, even, odd, tend)
 
     def step(chunk, total):
-        for group in range(10):
-            for half in range(2):
+        for half in range(2):
+            for group in range(10):
                 rows = slice(16 * half, 16 * half + 16)
                 place = slice(32 * chunk + 16 * half, 32 * chunk + 16 * half + 16)
                 if group < 8:
@@ -168,10 +168,13 @@
                     )
                 tile = jnp.swapaxes(tile, 0, 1)
                 for s in range(16):
-                    lanes = slice(256 * s + 128 * half, 256 * s + 128 * half + 128)
+                    lanes = slice(2048 * half + 128 * s, 2048 * half + 128 * s + 128)
                     turned_ref[chunk, 16 * group : 16 * group + 16, lanes] = tile[s]
-        block = turned_ref[chunk]
-        return total + lax.dot_general(block, block, contract_last, preferred_element_type=f32)
+            block = turned_ref[chunk, :, 2048 * half : 2048 * half + 2048]
+            total = total + lax.dot_general(
+                block, block, contract_last, preferred_element_type=f32
+            )
+        return total
 
     total = jnp.zeros((160, 160), f32)
     for chunk in range(6):
@@ -330,7 +333,10 @@
             for half in range(2):
                 tile = jnp.stack(
                     [
-                        total[16 * group : 16 * group + 16, 256 * s + 128 * half : 256 * s + 128 * half + 128]
+                        total[
+                            16 * group : 16 * group + 16,
+                            2048 * half + 128 * s : 2048 * half + 128 * s + 128,
+                        ]
                         for s in range(16)
                     ],
                     axis=0,

time: 71.9 us -> 71.6 us (level)
  no operation moved by 1% of the time
where the time goes in v4:
time: 71.6 us; the launch traced here: 71.3 us
  blocking collectives  36.6 us (51%)
  Pallas kernels  18.2 us (25%)
  starting transfers between devices  11.2 us (16%)
  local copies, waits for them, and re-layouts  2.74 us (4%)
  waiting for transfers between devices  1.7 us (2%)
  between operations  0.72 us (1%)
    all_to_all x2, blocking collectives, everyone(): return lax.all_to_all(copies, axis, 0, 0)  27 us
    ppermute x4, starting transfers between devices, neighbours(): return (lax.ppermute(last, axis, up), lax.ppermute(first, axis, down))  11.2 us
    all_to_all x1, blocking collectives, body(): mine = added(lax.all_to_all(packed.reshape(8, 1, -1), 'gx', 0, 0))  9.67 us
    pallas_call x1, Pallas kernels, finish(): pl.pallas_call(functools.partial(last_kernel, rows_total), in_specs=[whol...  8.65 us
    pallas_call x1, Pallas kernels, local_gram(): pl.pallas_call(gram_kernel, in_specs=[pl.BlockSpec(memory_space=pltpu.SME...  6.53 us
    pallas_call x1, Pallas kernels, loaded_parts(): pl.pallas_call(load_kernel, in_specs=[pl.BlockSpec(memory_space=pl.ANY)]...  2.98 us
    ppermute x4, waiting for transfers between devices, neighbours(): return (lax.ppermute(last, axis, up), lax.ppermute(first, axis, down))  1.7 us
    unnamed x6, local copies, waits for them, and re-layouts  1.55 us
  transfers between devices with their start and end apart: 4, of which 2 were waited for; matrix products, arithmetic and copies ran while one was open for 1% of the time, Pallas kernels for 4%

profile of v4, /device:TPU:1, one launch (start us, length us, event | category | flops | bytes accessed | tf_op | source)
XLA Modules:
  0.0 71.3 jit_solution(1584505081192390777)
XLA Ops:
  0.6 0.0 copy-start.2
  0.6 0.0 copy-start.1
  0.7 2.5 %collective-permute-start = (f32[3,8,8,128]{3,2,1,0:T(8,128)}, f32[3,8,8,128]{3,2,1,0:T(8,128)S(1)}, u32[]{:S(2)}, u32[]{:S(2)}) collective-permute-start(f32[3,8,8,128]{3,2,1,0:T(8,128)} %param.5), channel_id=1, source_target_pairs={{0,1},{1,2},{2,3},{3,4},{4,5},{5,6},{6,7},{7,8},{8,9},{9,10},{10,1... | collective-permute-start | bytes 294920 | tf_op jit(solution)/shard_map/ppermute | solution.py:21
  3.2 6.2 %collective-permute-start.1 = (f32[3,8,6,128]{3,2,1,0:T(8,128)}, f32[3,8,6,128]{3,2,1,0:T(8,128)S(1)}, u32[]{:S(2)}, u32[]{:S(2)}) collective-permute-start(f32[3,8,6,128]{3,2,1,0:T(8,128)} %bitcast.13), channel_id=1, source_target_pairs={{1,0},{2,1},{3,2},{4,3},{5,4},{6,5},{7,6},{8,7},{9,8},{10,9},{11,1... | collective-permute-start | bytes 221192 | tf_op jit(solution)/shard_map/ppermute | solution.py:21
  9.4 0.9 %pad.4.own_ref = f32[3,8,24,128]{3,2,1,0:T(8,128)S(1)} pad(f32[3,8,8,128]{3,2,1,0:T(8,128)} %param.5, f32[]{:T(128)} %constant.2.clone.1), padding=0_0x0_0x6_10x0_0 | pad | bytes 393220 | tf_op jit(solution)/shard_map/jit(_pad)/pad | solution.py:394
  10.4 1.0 %collective-permute-done.1.ahead_ref = f32[3,8,6,128]{3,2,1,0:T(8,128)S(1)} collective-permute-done((f32[3,8,6,128]{3,2,1,0:T(8,128)}, f32[3,8,6,128]{3,2,1,0:T(8,128)S(1)}, u32[]{:S(2)}, u32[]{:S(2)}) %collective-permute-start.1) | collective-permute-done | bytes 73760 | tf_op jit(solution)/shard_map/ppermute | solution.py:21
  11.4 0.7 collective-permute-done.behind_ref
  12.1 0.1 shard_map.77
  12.1 2.4 %collective-permute-start.2 = (f32[3,2,36,128]{3,2,1,0:T(8,128)S(1)}, f32[3,2,36,128]{3,2,1,0:T(8,128)S(1)}, u32[]{:S(2)}, u32[]{:S(2)}) collective-permute-start(f32[3,2,36,128]{3,2,1,0:T(8,128)S(1)} %get-tuple-element.16), channel_id=1, source_target_pairs={{0,32},{32,64},{64,96},{96,128},{128,160},{160,192},{192,224},{224... | collective-permute-start | bytes 331784 | tf_op jit(solution)/shard_map/ppermute | solution.py:21
  14.5 0.0 collective-permute-start.3
  14.5 0.0 copy-start
  14.5 1.5 %copy-done = bf16[40,3,8,8,128]{4,3,2,1,0:T(8,128)(2,1)S(1)} copy-done((bf16[40,3,8,8,128]{4,3,2,1,0:T(8,128)(2,1)S(1)}, bf16[40,3,8,8,128]{4,3,2,1,0:T(8,128)(2,1)}, u32[]{:S(2)}) %copy-start) | copy-done | bytes 1966104
  16.1 3.0 %shard_map.76 = (bf16[6,128,32,128]{3,2,1,0:T(8,128)(2,1)S(1)}, bf16[6,40,32,128]{3,2,1,0:T(8,128)(2,1)S(1)}) custom-call(bf16[128,192,128]{2,1,0:T(8,128)(2,1)} %bitcast.12, bf16[40,192,128]{2,1,0:T(8,128)(2,1)S(1)} %bitcast.9), custom_call_target="tpu_custom_call" | custom-call | bytes 16000000 | tf_op jit(solution)/shard_map/pallas_call | solution.py:130
  19.1 0.0 collective-permute-done.2.behind_ref
  19.1 0.0 collective-permute-done.3.ahead_ref
  19.1 0.0 copy-done.2
  19.1 0.0 copy-done.1
  19.1 6.5 %shard_map.78 = (f32[8,2048]{1,0:T(8,128)S(1)}, bf16[6,160,4096]{2,1,0:T(8,128)(2,1)S(1)}, f32[192,128]{1,0:T(8,128)}) custom-call(s32[31]{0:T(128)S(1)} %copy-done.2, bf16[6,128,32,128]{3,2,1,0:T(8,128)(2,1)S(1)} %get-tuple-element.13.basis_ref, bf16[6,40,32,128]{3,2,1,0:T(8,128)(2,1)S(1)} %get-tuple-element.14.stored_ref, f32[1,129]{1,0:T(1,128)S(1)} %bitcast.11, ...), custom_call_target="tpu_custom_call" | custom-call | flops 2000000000 | bytes 16000000 | tf_op jit(solution)/shard_map/pallas_call | solution.py:194
  25.6 0.1 copy.8
  25.7 9.7 %all_to_all.15 = f32[8,1,2048]{2,1,0:T(1,128)S(1)} all-to-all(f32[8,1,2048]{2,1,0:T(1,128)S(1)} %copy.8), channel_id=1, replica_groups=mesh['gx'=8,'gz'=32] {'gx'}, dimensions={0} | all-to-all | bytes 131072 | tf_op jit(solution)/shard_map/all_to_all | solution.py:405
  35.4 0.1 broadcast_in_dim.15
  35.6 16.1 %all_to_all.16 = f32[32,1,2048]{2,1,0:T(1,128)S(1)} all-to-all(f32[32,1,2048]{2,1,0:T(1,128)S(1)} %broadcast_in_dim.15), channel_id=1, replica_groups=mesh['gx'=8,'gz'=32] {'gz'}, dimensions={0} | all-to-all | bytes 524288 | tf_op jit(solution)/shard_map/all_to_all | solution.py:383
  51.7 0.1 slice_add_fusion
  51.8 10.9 %all_to_all.17.sums_ref = f32[8,1,2048]{2,1,0:T(1,128)S(1)} all-to-all(f32[8,1,2048]{2,1,0:T(1,128)S(1)} %broadcast_in_dim.17), channel_id=1, replica_groups=mesh['gx'=8,'gz'=32] {'gx'}, dimensions={0} | all-to-all | bytes 131072 | tf_op jit(solution)/shard_map/all_to_all | solution.py:383
  62.7 8.7 %shard_map.79 = (f32[160,160]{1,0:T(8,128)}, bf16[32,192,128]{2,1,0:T(8,128)(2,1)}) custom-call(f32[8,1,2048]{2,1,0:T(1,128)S(1)} %all_to_all.17.sums_ref, bf16[6,160,4096]{2,1,0:T(8,128)(2,1)S(1)} %get-tuple-element.20.turned_ref), custom_call_target="tpu_custom_call" | custom-call | tf_op jit(solution)/shard_map/pallas_call | solution.py:360
  (2 shorter events, 0.1 us)
Async XLA Ops:
  0.6 18.5 %copy-start.2 = (s32[31]{0:T(128)S(1)}, s32[31]{0:T(128)}, u32[]{:S(2)}) copy-start(s32[31]{0:T(128)} %picks_ref.1) | copy-start | bytes 376
  0.6 18.5 %copy-start.1 = (f32[129]{0:T(256)S(1)}, f32[129]{0:T(256)}, u32[]{:S(2)}) copy-start(f32[129]{0:T(256)} %param.6) | copy-start | bytes 1552
  0.7 11.4 %collective-permute-start = (f32[3,8,8,128]{3,2,1,0:T(8,128)}, f32[3,8,8,128]{3,2,1,0:T(8,128)S(1)}, u32[]{:S(2)}, u32[]{:S(2)}) collective-permute-start(f32[3,8,8,128]{3,2,1,0:T(8,128)} %param.5), channel_id=1, source_target_pairs={{0,1},{1,2},{2,3},{3,4},{4,5},{5,6},{6,7},{7,8},{8,9},{9,10},{10,1... | collective-permute-start | bytes 294920 | tf_op jit(solution)/shard_map/ppermute | solution.py:21
  3.2 8.2 %collective-permute-start.1 = (f32[3,8,6,128]{3,2,1,0:T(8,128)}, f32[3,8,6,128]{3,2,1,0:T(8,128)S(1)}, u32[]{:S(2)}, u32[]{:S(2)}) collective-permute-start(f32[3,8,6,128]{3,2,1,0:T(8,128)} %bitcast.13), channel_id=1, source_target_pairs={{1,0},{2,1},{3,2},{4,3},{5,4},{6,5},{7,6},{8,7},{9,8},{10,9},{11,1... | collective-permute-start | bytes 221192 | tf_op jit(solution)/shard_map/ppermute | solution.py:21
  12.1 7.0 %collective-permute-start.2 = (f32[3,2,36,128]{3,2,1,0:T(8,128)S(1)}, f32[3,2,36,128]{3,2,1,0:T(8,128)S(1)}, u32[]{:S(2)}, u32[]{:S(2)}) collective-permute-start(f32[3,2,36,128]{3,2,1,0:T(8,128)S(1)} %get-tuple-element.16), channel_id=1, source_target_pairs={{0,32},{32,64},{64,96},{96,128},{128,160},{160,192},{192,224},{224... | collective-permute-start | bytes 331784 | tf_op jit(solution)/shard_map/ppermute | solution.py:21
  14.5 4.5 %collective-permute-start.3 = (f32[3,2,36,128]{3,2,1,0:T(8,128)S(1)}, f32[3,2,36,128]{3,2,1,0:T(8,128)S(1)}, u32[]{:S(2)}, u32[]{:S(2)}) collective-permute-start(f32[3,2,36,128]{3,2,1,0:T(8,128)S(1)} %get-tuple-element.17), channel_id=1, source_target_pairs={{32,0},{64,32},{96,64},{128,96},{160,128},{192,160},{224,192},{0,2... | collective-permute-start | bytes 331784 | tf_op jit(solution)/shard_map/ppermute | solution.py:21
  14.5 1.5 %copy-start = (bf16[40,3,8,8,128]{4,3,2,1,0:T(8,128)(2,1)S(1)}, bf16[40,3,8,8,128]{4,3,2,1,0:T(8,128)(2,1)}, u32[]{:S(2)}) copy-start(bf16[40,3,8,8,128]{4,3,2,1,0:T(8,128)(2,1)} %param.8) | copy-start | bytes 5898244
